TPU v7x, 128 devices: a whole 4x4x4 slice. The times are simulated.
128 devices in a mesh: dp: 32 (over x, z, core), outer: 4 (over y).
Axes of the slice: x: 4, y: 4, z: 4, core: 2. Of those that a mesh axis runs over, the one named last changes fastest.
Arguments:
- tokens_in: bfloat16 [49152, 960], P(('dp', 'outer')), may hold values from -16 to 16
- segment_ids: int32 [49152], P(('dp', 'outer')), may hold values from 0 to 4, as said below
- norm_in: bfloat16 [960], P('dp'), may hold values from 0.099609375 to 1.8984375
- w_query: bfloat16 [960, 960], P('dp'), may hold values from -0.1875 to 0.1875
- w_key: bfloat16 [960, 320], P('dp'), may hold values from -0.1875 to 0.1875
- w_value: bfloat16 [960, 320], P('dp'), may hold values from -0.1875 to 0.1875
- w_out: bfloat16 [960, 960], P('dp'), may hold values from -0.75 to 0.75
- norm_mid: bfloat16 [960], P('dp'), may hold values from 0.099609375 to 1.8984375
- w_gate: bfloat16 [960, 2560], P('dp'), may hold values from -0.1875 to 0.1875
- w_up: bfloat16 [960, 2560], P('dp'), may hold values from -0.1875 to 0.1875
- w_down: bfloat16 [2560, 960], P('dp'), may hold values from -0.125 to 0.125
- out_cotangent: bfloat16 [49152, 960], P(('dp', 'outer')), may hold values from -6 to 6
Outputs:
- layer_out: bfloat16 [49152, 960], P(('dp', 'outer'))
- grad_input: bfloat16 [49152, 960], P(('dp', 'outer'))
- grad_norm_in: float32 [960], P('dp')
- grad_query: float32 [960, 960], P('dp')
- grad_key: float32 [960, 320], P('dp')
- grad_value: float32 [960, 320], P('dp')
- grad_out: float32 [960, 960], P('dp')
- grad_norm_mid: float32 [960], P('dp')
- grad_gate: float32 [960, 2560], P('dp')
- grad_up: float32 [960, 2560], P('dp')
- grad_down: float32 [2560, 960], P('dp')
Inputs may be any that keep to these rules, and one draw needn't show every extreme that they name: `segment_ids`: within each aligned block of 128 slots the ids never fall and start live at slot 0; 4 marks padding, which fills the end of a block; every block has half of its slots or more live, some blocks are full and some half padding.
All inputs are finite; a program needn't handle non-finite values.
Results may differ from a plain program's by a relative error of at most 0.028.
Values may be sent and summed in bfloat16 or wider, within the bound.
No kernel may reach another device: no remote copies, remote signals or barrier semaphores. Data moves between devices by JAX's collectives and lax.ppermute only.
A program may use at most 256 MiB of HBM per device.

v0:
```python
import math

import jax
import jax.numpy as jnp
from jax import lax
from jax.sharding import PartitionSpec as P

HEADS = 15
KV_HEADS = 5
HEAD_DIM = 64
MB_ROWS = 128
DOCS = 4


EPSILON = 1e-05
ROPE_BASE = 100000.0


def rms_scale(values):
    return lax.rsqrt(jnp.mean(values * values, axis=-1, keepdims=True) + EPSILON)


def rotate(values, cosine, sine):
    middle = values.shape[-1] // 2
    first_half = values[..., :middle]
    second_half = values[..., middle:]
    return jnp.concatenate(
        [first_half * cosine - second_half * sine, second_half * cosine + first_half * sine],
        axis=-1,
    )


def rope_tables(segment):
    span_size = segment.shape[-1]
    index = jnp.arange(span_size, dtype=jnp.int32)
    change = jnp.concatenate([jnp.ones((1,), dtype=bool), segment[1:] != segment[:-1]], axis=-1)
    starts = lax.cummax(jnp.where(change, index, 0), axis=0)
    offset = (index - starts).astype(jnp.float32)
    inverse_freq = jnp.exp(
        jnp.arange(HEAD_DIM // 2, dtype=jnp.float32) * (-2.0 * math.log(ROPE_BASE) / HEAD_DIM)
    )
    angles = offset[:, None] * inverse_freq
    return (jnp.cos(angles)[:, None, :], jnp.sin(angles)[:, None, :])


def inner_rows(left, right):
    return lax.dot_general(
        left, right, (((0,), (0,)), ((), ())), preferred_element_type=jnp.float32
    )


def times_transposed(left, right):
    return lax.dot_general(
        left, right, (((1,), (1,)), ((), ())), preferred_element_type=jnp.float32
    )


def product(left, right):
    return jnp.dot(left, right, preferred_element_type=jnp.float32)


def forward_block(weights_full, inputs, segment):
    norm_in, w_query, w_key, w_value, w_out, norm_mid, w_gate, w_up, w_down = weights_full
    row_count = inputs.shape[0]
    share = HEADS // KV_HEADS
    cosine, sine = rope_tables(segment)
    index = jnp.arange(row_count, dtype=jnp.int32)
    allowed = (segment[:, None] == segment[None, :]) & (index[:, None] >= index[None, :])
    live_rows = (segment < DOCS).astype(jnp.float32)[:, None]
    x_float = inputs.astype(jnp.float32)
    scale_in = rms_scale(x_float)
    normed_in = (x_float * scale_in * norm_in.astype(jnp.float32)).astype(jnp.bfloat16)
    query_raw = product(normed_in, w_query).reshape(row_count, HEADS, HEAD_DIM)
    key_raw = product(normed_in, w_key).reshape(row_count, KV_HEADS, HEAD_DIM)
    value_low = (
        product(normed_in, w_value).astype(jnp.bfloat16).reshape(row_count, KV_HEADS, HEAD_DIM)
    )
    query_low = (
        rotate(query_raw, cosine, sine)
        .astype(jnp.bfloat16)
        .reshape(row_count, KV_HEADS, share, HEAD_DIM)
    )
    key_low = rotate(key_raw, cosine, sine).astype(jnp.bfloat16)
    scores = jnp.einsum(
        "rksd,tkd->ksrt", query_low, key_low, preferred_element_type=jnp.float32
    ) * HEAD_DIM ** (-0.5)
    scores = jnp.where(allowed[None, None], scores, -1e30)
    probs = jnp.exp(scores - jnp.max(scores, axis=-1, keepdims=True))
    probs = probs / jnp.sum(probs, axis=-1, keepdims=True)
    probs_low = probs.astype(jnp.bfloat16)
    mixed = jnp.einsum("ksrt,tkd->rksd", probs_low, value_low, preferred_element_type=jnp.float32)
    mixed = mixed.reshape(row_count, HEADS * HEAD_DIM).astype(jnp.bfloat16)
    after_attn = x_float + product(mixed, w_out)
    scale_mid = rms_scale(after_attn)
    normed_mid = (after_attn * scale_mid * norm_mid.astype(jnp.float32)).astype(jnp.bfloat16)
    gate_pre = product(normed_mid, w_gate)
    up_pre = product(normed_mid, w_up)
    hidden = (jax.nn.silu(gate_pre) * up_pre).astype(jnp.bfloat16)
    result = ((after_attn + product(hidden, w_down)) * live_rows).astype(jnp.bfloat16)
    saved = (
        x_float,
        scale_in,
        normed_in,
        cosine,
        sine,
        allowed,
        live_rows,
        value_low,
        query_low,
        key_low,
        probs,
        probs_low,
        mixed,
        after_attn,
        scale_mid,
        normed_mid,
        gate_pre,
        up_pre,
        hidden,
    )
    return (result, saved)


def backward_block(weights_full, saved, cotangent):
    norm_in, w_query, w_key, w_value, w_out, norm_mid, w_gate, w_up, w_down = weights_full
    (
        x_float,
        scale_in,
        normed_in,
        cosine,
        sine,
        allowed,
        live_rows,
        value_low,
        query_low,
        key_low,
        probs,
        probs_low,
        mixed,
        after_attn,
        scale_mid,
        normed_mid,
        gate_pre,
        up_pre,
        hidden,
    ) = saved
    row_count = x_float.shape[0]
    share = HEADS // KV_HEADS
    head_scale = HEAD_DIM ** (-0.5)
    grad_result = cotangent.astype(jnp.float32) * live_rows
    grad_result_low = grad_result.astype(jnp.bfloat16)
    grad_down = inner_rows(hidden, grad_result_low)
    grad_hidden = times_transposed(grad_result_low, w_down)
    sigmoid_gate = jax.nn.sigmoid(gate_pre)
    grad_gate_pre = (
        grad_hidden * up_pre * sigmoid_gate * (1.0 + gate_pre * (1.0 - sigmoid_gate))
    ).astype(jnp.bfloat16)
    grad_up_pre = (grad_hidden * (gate_pre * sigmoid_gate)).astype(jnp.bfloat16)
    grad_gate = inner_rows(normed_mid, grad_gate_pre)
    grad_up = inner_rows(normed_mid, grad_up_pre)
    grad_normed_mid = times_transposed(grad_gate_pre, w_gate) + times_transposed(grad_up_pre, w_up)
    grad_norm_mid = jnp.sum(grad_normed_mid * after_attn * scale_mid, axis=0)
    grad_scaled_mid = grad_normed_mid * norm_mid.astype(jnp.float32)
    grad_after = (
        grad_result
        + scale_mid * grad_scaled_mid
        - after_attn * scale_mid**3 * jnp.mean(grad_scaled_mid * after_attn, axis=-1, keepdims=True)
    )
    grad_after_low = grad_after.astype(jnp.bfloat16)
    grad_out = inner_rows(mixed, grad_after_low)
    grad_mixed = (
        times_transposed(grad_after_low, w_out)
        .astype(jnp.bfloat16)
        .reshape(row_count, KV_HEADS, share, HEAD_DIM)
    )
    grad_probs = jnp.einsum(
        "rksd,tkd->ksrt", grad_mixed, value_low, preferred_element_type=jnp.float32
    )
    grad_value_low = jnp.einsum(
        "ksrt,rksd->tkd", probs_low, grad_mixed, preferred_element_type=jnp.float32
    )
    grad_value_low = grad_value_low.astype(jnp.bfloat16).reshape(row_count, KV_HEADS * HEAD_DIM)
    row_delta = jnp.sum(probs * grad_probs, axis=-1, keepdims=True)
    grad_scores = jnp.where(allowed[None, None], probs * (grad_probs - row_delta), 0.0).astype(
        jnp.bfloat16
    )
    grad_query_rot = (
        jnp.einsum("ksrt,tkd->rksd", grad_scores, key_low, preferred_element_type=jnp.float32)
        * head_scale
    )
    grad_key_rot = (
        jnp.einsum("ksrt,rksd->tkd", grad_scores, query_low, preferred_element_type=jnp.float32)
        * head_scale
    )
    grad_query_low = rotate(grad_query_rot.reshape(row_count, HEADS, HEAD_DIM), cosine, -sine)
    grad_query_low = grad_query_low.astype(jnp.bfloat16).reshape(row_count, HEADS * HEAD_DIM)
    grad_key_low = (
        rotate(grad_key_rot, cosine, -sine)
        .astype(jnp.bfloat16)
        .reshape(row_count, KV_HEADS * HEAD_DIM)
    )
    grad_query = inner_rows(normed_in, grad_query_low)
    grad_key = inner_rows(normed_in, grad_key_low)
    grad_value = inner_rows(normed_in, grad_value_low)
    grad_normed_in = (
        times_transposed(grad_query_low, w_query)
        + times_transposed(grad_key_low, w_key)
        + times_transposed(grad_value_low, w_value)
    )
    grad_norm_in = jnp.sum(grad_normed_in * x_float * scale_in, axis=0)
    grad_scaled_in = grad_normed_in * norm_in.astype(jnp.float32)
    grad_inputs = (
        grad_after
        + scale_in * grad_scaled_in
        - x_float * scale_in**3 * jnp.mean(grad_scaled_in * x_float, axis=-1, keepdims=True)
    )
    weight_grads = (
        grad_norm_in,
        grad_query,
        grad_key,
        grad_value,
        grad_out,
        grad_norm_mid,
        grad_gate,
        grad_up,
        grad_down,
    )
    return (weight_grads, grad_inputs.astype(jnp.bfloat16))


def add_tuples(first, second):
    return tuple((left + right for left, right in zip(first, second)))


def local(
    tokens_in,
    segment_ids,
    norm_in,
    w_query,
    w_key,
    w_value,
    w_out,
    norm_mid,
    w_gate,
    w_up,
    w_down,
    out_cotangent,
):
    batch_count = tokens_in.shape[0] // MB_ROWS
    results = []
    grads_in = []
    totals = None
    for batch_index in range(batch_count):
        lower = batch_index * MB_ROWS
        inputs = tokens_in[lower : lower + MB_ROWS]
        segment = segment_ids[lower : lower + MB_ROWS]
        cotangent = out_cotangent[lower : lower + MB_ROWS]
        gathered = (
            lax.all_gather(norm_in, "dp", axis=0, tiled=True),
            lax.all_gather(w_query, "dp", axis=0, tiled=True),
            lax.all_gather(w_key, "dp", axis=0, tiled=True),
            lax.all_gather(w_value, "dp", axis=0, tiled=True),
            lax.all_gather(w_out, "dp", axis=0, tiled=True),
            lax.all_gather(norm_mid, "dp", axis=0, tiled=True),
            lax.all_gather(w_gate, "dp", axis=0, tiled=True),
            lax.all_gather(w_up, "dp", axis=0, tiled=True),
            lax.all_gather(w_down, "dp", axis=0, tiled=True),
        )
        result, saved = forward_block(gathered, inputs, segment)
        again = (
            lax.all_gather(norm_in, "dp", axis=0, tiled=True),
            lax.all_gather(w_query, "dp", axis=0, tiled=True),
            lax.all_gather(w_key, "dp", axis=0, tiled=True),
            lax.all_gather(w_value, "dp", axis=0, tiled=True),
            lax.all_gather(w_out, "dp", axis=0, tiled=True),
            lax.all_gather(norm_mid, "dp", axis=0, tiled=True),
            lax.all_gather(w_gate, "dp", axis=0, tiled=True),
            lax.all_gather(w_up, "dp", axis=0, tiled=True),
            lax.all_gather(w_down, "dp", axis=0, tiled=True),
        )
        weight_grads, grad_inputs = backward_block(again, saved, cotangent)
        results.append(result)
        grads_in.append(grad_inputs)
        totals = weight_grads if totals is None else add_tuples(totals, weight_grads)
    g_norm_in, g_query, g_key, g_value, g_out, g_norm_mid, g_gate, g_up, g_down = totals
    totals = (
        lax.psum_scatter(
            g_norm_in.astype(jnp.bfloat16), "dp", scatter_dimension=0, tiled=True
        ).astype(jnp.float32),
        lax.psum_scatter(
            g_query.astype(jnp.bfloat16), "dp", scatter_dimension=0, tiled=True
        ).astype(jnp.float32),
        lax.psum_scatter(g_key.astype(jnp.bfloat16), "dp", scatter_dimension=0, tiled=True).astype(
            jnp.float32
        ),
        lax.psum_scatter(
            g_value.astype(jnp.bfloat16), "dp", scatter_dimension=0, tiled=True
        ).astype(jnp.float32),
        lax.psum_scatter(g_out.astype(jnp.bfloat16), "dp", scatter_dimension=0, tiled=True).astype(
            jnp.float32
        ),
        lax.psum_scatter(
            g_norm_mid.astype(jnp.bfloat16), "dp", scatter_dimension=0, tiled=True
        ).astype(jnp.float32),
        lax.psum_scatter(g_gate.astype(jnp.bfloat16), "dp", scatter_dimension=0, tiled=True).astype(
            jnp.float32
        ),
        lax.psum_scatter(g_up.astype(jnp.bfloat16), "dp", scatter_dimension=0, tiled=True).astype(
            jnp.float32
        ),
        lax.psum_scatter(g_down.astype(jnp.bfloat16), "dp", scatter_dimension=0, tiled=True).astype(
            jnp.float32
        ),
    )
    s_norm_in, s_query, s_key, s_value, s_out, s_norm_mid, s_gate, s_up, s_down = totals
    summed = (
        lax.psum(s_norm_in.astype(jnp.bfloat16), "outer").astype(jnp.float32),
        lax.psum(s_query.astype(jnp.bfloat16), "outer").astype(jnp.float32),
        lax.psum(s_key.astype(jnp.bfloat16), "outer").astype(jnp.float32),
        lax.psum(s_value.astype(jnp.bfloat16), "outer").astype(jnp.float32),
        lax.psum(s_out.astype(jnp.bfloat16), "outer").astype(jnp.float32),
        lax.psum(s_norm_mid.astype(jnp.bfloat16), "outer").astype(jnp.float32),
        lax.psum(s_gate.astype(jnp.bfloat16), "outer").astype(jnp.float32),
        lax.psum(s_up.astype(jnp.bfloat16), "outer").astype(jnp.float32),
        lax.psum(s_down.astype(jnp.bfloat16), "outer").astype(jnp.float32),
    )
    layer_out = jnp.concatenate(results, axis=0)
    grad_input = jnp.concatenate(grads_in, axis=0)
    return (layer_out, grad_input) + tuple(summed)


def solution(mesh):
    in_specs = (
        P(("dp", "outer"), None),
        P(("dp", "outer")),
        P("dp"),
        P("dp", None),
        P("dp", None),
        P("dp", None),
        P("dp", None),
        P("dp"),
        P("dp", None),
        P("dp", None),
        P("dp", None),
        P(("dp", "outer"), None),
    )
    out_specs = (
        P(("dp", "outer"), None),
        P(("dp", "outer"), None),
        P("dp"),
        P("dp", None),
        P("dp", None),
        P("dp", None),
        P("dp", None),
        P("dp"),
        P("dp", None),
        P("dp", None),
        P("dp", None),
    )
    return jax.shard_map(local, mesh=mesh, in_specs=in_specs, out_specs=out_specs, check_vma=False)
```

profile of v0, /device:TPU:0, one launch (start us, length us, event | category | flops | bytes accessed | tf_op | source)
XLA Modules:
  0.0 736.7 jit_solution(17012535673079227443)
XLA Ops:
  10.6 26.3 %all-gather = bf16[32,30,320]{2,1,0:T(8,128)(2,1)S(1)} all-gather(bf16[1,30,320]{2,1,0:T(8,128)(2,1)} %bitcast.447), channel_id=1, replica_groups=mesh['dp'=32,'outer'=4] {'dp'}, dimensions={0}, use_global_device_ids=true | all-gather | bytes 633600 | tf_op jit(solution)/shard_map/all_gather | solution.py:262
  39.3 24.2 %all-gather.1 = bf16[32,30,320]{2,1,0:T(8,128)(2,1)S(1)} all-gather(bf16[1,30,320]{2,1,0:T(8,128)(2,1)S(1)} %bitcast.448), channel_id=1, replica_groups=mesh['dp'=32,'outer'=4] {'dp'}, dimensions={0}, use_global_device_ids=true | all-gather | bytes 633600 | tf_op jit(solution)/shard_map/all_gather | solution.py:261
  65.9 65.5 %all-reduce.17 = (bf16[960]{0:T(1024)(128)(2,1)S(1)}, bf16[960]{0:T(1024)(128)(2,1)S(1)}) all-reduce(bf16[960]{0:T(1024)(128)(2,1)S(1)} %dynamic-update-slice, bf16[960]{0:T(1024)(128)(2,1)S(1)} %dynamic-update-slice.1), channel_id=1, replica_groups=mesh['dp'=32,'outer'=4] {'dp'}, use_global_device_ids=true, to_apply=%add | all-reduce | flops 1920 | bytes 7680
  144.0 4.0 reshape.760
  148.0 3.1 reshape.762
  151.2 2.6 fusion.200
  165.9 2.8 multiply_reduce_fusion.10
  175.9 2.6 multiply_reduce_fusion.9
  180.0 7.5 %reshape.764 = bf16[960,2560]{1,0:T(8,128)(2,1)} reshape(bf16[32,30,2560]{2,1,0:T(8,128)(2,1)} %all-gather.18.cloned.1.call-done) | data formatting | bytes 9830400
  187.5 12.9 %all-gather.20.cloned.1.call-done = bf16[32,30,2560]{2,1,0:T(8,128)(2,1)} async-done(((bf16[1,30,2560]{2,1,0:T(8,128)(2,1)}), bf16[32,30,2560]{2,1,0:T(8,128)(2,1)}) %all-gather.20.cloned.1.call-update) | async-done | bytes 4915216 | tf_op jit(solution)/shard_map/all_gather | solution.py:266
  200.4 7.9 %reshape.766 = bf16[960,2560]{1,0:T(8,128)(2,1)} reshape(bf16[32,30,2560]{2,1,0:T(8,128)(2,1)} %all-gather.20.cloned.1.call-done) | data formatting | bytes 9830400
  208.2 4.5 fusion.211
  214.7 34.6 %all-gather.12.cloned.1.call-done = bf16[2560,960]{1,0:T(8,128)(2,1)} async-done(((bf16[80,960]{1,0:T(8,128)(2,1)}), bf16[2560,960]{1,0:T(8,128)(2,1)}) %all-gather.12.cloned.1.call-update) | async-done | bytes 4915216 | tf_op jit(solution)/shard_map/all_gather | solution.py:267
  249.3 6.4 multiply_convert_fusion.4
  257.4 4.4 multiply_reduce_fusion.5
  263.9 3.0 multiply_convert_fusion.2
  278.9 3.3 fusion.49
  282.1 3.4 convolution_multiply_fusion.5
  290.6 3.3 fusion.51
  294.0 3.4 convolution_multiply_fusion.4
  297.4 6.5 multiply_convert_fusion
  305.4 3.9 multiply_reduce_fusion.3
  314.0 2.7 fusion.53
  316.7 2.8 convolution_multiply_fusion.3
  319.5 2.6 fusion.133
  322.1 2.6 fusion.130
  324.7 5.5 fusion.220
  330.2 5.2 fusion.221
  335.4 5.1 fusion.222
  340.5 5.2 fusion.223
  346.9 2.7 fusion.198
  349.6 2.6 fusion.187
  360.1 5.5 fusion.121
  365.7 8.1 %add_convert_fusion = bf16[2560,960]{1,0:T(8,128)(2,1)} fusion(f32[2560,960]{1,0:T(8,128)S(1)} %fusion.117, f32[2560,960]{1,0:T(8,128)} %fusion.121, bf16[128,2560]{1,0:T(8,128)(2,1)S(1)} %copy-done.52, f32[128]{0:T(128)S(1)} %copy-done.129, bf16[384,960]{0,1:T(8,128)(2,1)S(1)} %copy-done.40), kind=kOutput, calls=%fused_computation.6 | convolution fusion | flops 636887040 | bytes 26132992 | tf_op jit(solution)/shard_map/dot_general | solution.py:47
  374.9 5.4 add_convert_fusion.3
  380.3 11.1 %add_convert_fusion.2 = bf16[960,2560]{1,0:T(8,128)(2,1)} fusion(f32[960,2560]{1,0:T(8,128)} %fusion.220, f32[960,2560]{1,0:T(8,128)} %fusion.221, bf16[128,960]{0,1:T(8,128)(2,1)S(1)} %copy-done.32, bf16[128,2560]{1,0:T(8,128)(2,1)S(1)} %copy-done.45), kind=kOutput, calls=%fused_computation.8 | convolution fusion | flops 636518400 | bytes 25477120 | tf_op jit(solution)/shard_map/dot_general | solution.py:47
  391.5 5.8 add_convert_fusion.4
  397.3 4.2 add_convert_fusion.6
  402.9 4.8 add_convert_fusion.1
  407.7 107.4 %fusion.205 = (bf16[32,960]{1,0:T(8,128)(2,1)}, bf16[32,320]{1,0:T(8,128)(2,1)}, bf16[32,320]{1,0:T(8,128)(2,1)S(1)}, bf16[32,960]{1,0:T(8,128)(2,1)S(1)}, bf16[...) fusion(bf16[960,960]{1,0:T(8,128)(2,1)} %add_convert_fusion.4, bf16[960,320]{1,0:T(8,128)(2,1)} %add_convert_fusion.6, ...), kind=kCustom, calls=%all-reduce-scatter.6 | all-reduce-scatter fusion | flops 7864321 | bytes 15237632
  524.8 3.1 collective-permute-start.5
  544.2 65.8 %all-reduce.16 = (bf16[960]{0:T(1024)(128)(2,1)S(1)}, bf16[960]{0:T(1024)(128)(2,1)S(1)}) all-reduce(bf16[960]{0:T(1024)(128)(2,1)S(1)} %add_convert_fusion.20, bf16[960]{0:T(1024)(128)(2,1)S(1)} %add_convert_fusion.19), channel_id=2, replica_groups=mesh['dp'=32,'outer'=4] {'dp'}, use_global_device_ids=true, to_apply=%region_27.28.clone | all-reduce | flops 1920 | bytes 7680
  623.4 3.1 collective-permute-start.7
  630.9 2.6 collective-permute-start.11
  634.7 5.4 concatenate.135
  641.9 6.4 concatenate.136
  654.6 24.6 %all-reduce.24.cloned.1.call-done = (bf16[30]{0:T(256)(128)(2,1)}, bf16[30,960]{1,0:T(8,128)(2,1)}, bf16[30,320]{1,0:T(8,128)(2,1)}, bf16[30,320]{1,0:T(8,128)(2...) async-done(((bf16[30]{0:T(256)(128)(2,1)}, bf16[30,960]{1,0:T(8,128)(2,1)}, bf16[30,320]{1,0:T(8,128)(2,1)}, bf16[30,320]{1,0:T(8,128)(2,1)}, bf16[30,960]{1,0:T(8,128)(2,1)}, ...) | async-done | bytes 153736 | tf_op jit(solution)/shard_map/psum | solution.py:317
  687.2 37.4 %all-reduce.26.cloned.1.call-done = (bf16[30,2560]{1,0:T(8,128)(2,1)}, bf16[30,2560]{1,0:T(8,128)(2,1)}, bf16[80,960]{1,0:T(8,128)(2,1)}) async-done(((bf16[30,2560]{1,0:T(8,128)(2,1)}, bf16[30,2560]{1,0:T(8,128)(2,1)}, bf16[80,960]{1,0:T(8,128)(2,1)}), (bf16[30,2560]{1,0:T(8,128)(2,1)}, bf16[30,2560]{1,0:T(8,128)(2,1)}, bf16[80,960]{1,0:T(8,128)(2,1)})) %all-reduce.26.cloned.1.call-update) | async-done | bytes 460816 | tf_op jit(solution)/shard_map/psum | solution.py:323
  (536 shorter events, 144.6 us)
Async XLA Ops:
  7.2 32.1 %copy-start.111 = (bf16[30,320]{1,0:T(8,128)(2,1)S(1)}, bf16[30,320]{1,0:T(8,128)(2,1)}, u32[]{:S(2)}) copy-start(bf16[30,320]{1,0:T(8,128)(2,1)} %param.16) | copy-start | bytes 57604
  7.2 56.3 %copy-start.4 = (bf16[384,960]{0,1:T(8,128)(2,1)S(1)}, bf16[384,960]{0,1:T(8,128)(2,1)}, u32[]{:S(2)}) copy-start(bf16[384,960]{0,1:T(8,128)(2,1)} %param.12) | copy-start | bytes 2211844
  7.2 136.8 %all-gather.14.cloned.1.call-start = ((), (), s32[]{:S(2)}) async-start(), calls=%async_computation.3 | async-start | bytes 2162688 | tf_op jit(solution)/shard_map/all_gather | solution.py:260
  7.9 140.1 %all-gather.16.cloned.1.call-start = ((), (), s32[]{:S(2)}) async-start(), calls=%async_computation.4 | async-start | bytes 2162688 | tf_op jit(solution)/shard_map/all_gather | solution.py:263
  8.7 171.3 %all-gather.18.cloned.1.call-start = ((), (), s32[]{:S(2)}) async-start(), calls=%async_computation.5 | async-start | bytes 5406720 | tf_op jit(solution)/shard_map/all_gather | solution.py:265
  9.4 190.9 %all-gather.20.cloned.1.call-start = ((), (), s32[]{:S(2)}) async-start(), calls=%async_computation.6 | async-start | bytes 5406720 | tf_op jit(solution)/shard_map/all_gather | solution.py:266
  10.0 239.3 %all-gather.12.cloned.1.call-start = ((), (), s32[]{:S(2)}) async-start(), calls=%async_computation.1 | async-start | bytes 5406720 | tf_op jit(solution)/shard_map/all_gather | solution.py:267
  10.6 639.3 %reduce-scatter.14.cloned.1.call-start = ((), (), s32[]{:S(2)}) async-start(), calls=%async_computation.2 | async-start | bytes 5406720 | tf_op jit(solution)/shard_map/reduce_scatter | solution.py:311
  36.9 27.2 %copy-start.136 = (u32[128]{0:T(128)S(1)}, u32[128]{0:T(128)}, u32[]{:S(2)}) copy-start(u32[128]{0:T(128)} %constant.59) | copy-start | bytes 1540
  37.9 27.6 %copy-start.146 = (bf16[30]{0:T(256)(128)(2,1)S(1)}, bf16[30]{0:T(256)(128)(2,1)}, u32[]{:S(2)}) copy-start(bf16[30]{0:T(256)(128)(2,1)} %param.14) | copy-start | bytes 184
  38.0 27.7 %copy-start.147 = (bf16[30]{0:T(256)(128)(2,1)S(1)}, bf16[30]{0:T(256)(128)(2,1)}, u32[]{:S(2)}) copy-start(bf16[30]{0:T(256)(128)(2,1)} %param.19) | copy-start | bytes 184
  63.5 70.7 %copy-start.112 = (s32[384]{0:T(512)S(1)}, s32[384]{0:T(512)}, u32[]{:S(2)}) copy-start(s32[384]{0:T(512)} %param.13) | copy-start | bytes 4612
  64.0 78.7 %copy-start.13 = (bf16[960,320]{1,0:T(8,128)(2,1)}, bf16[960,320]{1,0:T(8,128)(2,1)S(1)}, u32[]{:S(2)}) copy-start(bf16[960,320]{1,0:T(8,128)(2,1)S(1)} %reshape.756) | copy-start | bytes 1843204
  158.7 20.3 %copy-start.5 = (f32[128,960]{0,1:T(8,128)}, f32[128,960]{0,1:T(8,128)S(1)}, u32[]{:S(2)}) copy-start(f32[128,960]{0,1:T(8,128)S(1)} %get-tuple-element.139) | copy-start | bytes 1474564
  159.3 19.8 %copy-start.133 = (f32[128]{0:T(128)}, f32[128]{0:T(128)S(1)}, u32[]{:S(2)}) copy-start(f32[128]{0:T(128)S(1)} %get-tuple-element.129) | copy-start | bytes 1540
  187.5 20.8 %copy-start.26 = (bf16[128,960]{0,1:T(8,128)(2,1)S(1)}, bf16[128,960]{0,1:T(8,128)(2,1)}, u32[]{:S(2)}) copy-start(bf16[128,960]{0,1:T(8,128)(2,1)} %multiply_convert_fusion.11) | copy-start | bytes 737284
  212.7 36.6 %copy-start.122 = (f32[128]{0:T(128)S(1)}, f32[128]{0:T(128)}, u32[]{:S(2)}) copy-start(f32[128]{0:T(128)} %get-tuple-element.95) | copy-start | bytes 1540
  212.7 43.0 %slice-start = ((s8[4915200]{0:T(1024)(128)(4,1)}), s8[720896]{0:T(1024)(128)(4,1)S(1)}, s32[]{:S(2)}) async-start(s8[4915200]{0:T(1024)(128)(4,1)} %bitcast.360), calls=%async_computation.9 | async-start | bytes 1441792
  373.8 305.4 %all-reduce.24.cloned.1.call-start = ((), (), s32[]{:S(2)}) async-start(), calls=%async_computation.7 | async-start | bytes 362496 | tf_op jit(solution)/shard_map/psum | solution.py:317
  374.1 23.2 %copy-start.69 = (bf16[128,5,64]{0,2,1:T(8,128)(2,1)}, bf16[128,5,64]{0,2,1:T(8,128)(2,1)S(1)}, u32[]{:S(2)}) copy-start(bf16[128,5,64]{0,2,1:T(8,128)(2,1)S(1)} %pad_maximum_fusion.22) | copy-start | bytes 245764
  374.9 16.6 %copy-start.64 = (bf16[128,15,64]{0,2,1:T(8,128)(2,1)}, bf16[128,15,64]{0,2,1:T(8,128)(2,1)S(1)}, u32[]{:S(2)}) copy-start(bf16[128,15,64]{0,2,1:T(8,128)(2,1)S(1)} %pad_maximum_fusion.7) | copy-start | bytes 737284
  380.3 22.5 %slice-start.13 = ((s8[9830400]{0:T(1024)(128)(4,1)}), s8[4194304]{0:T(1024)(128)(4,1)S(1)}, s32[]{:S(2)}) async-start(s8[9830400]{0:T(1024)(128)(4,1)} %bitcast.372), calls=%async_computation.22 | async-start | bytes 8388608
  380.3 22.5 %slice-start.14 = ((s8[9830400]{0:T(1024)(128)(4,1)}), s8[4194304]{0:T(1024)(128)(4,1)S(1)}, s32[]{:S(2)}) async-start(s8[9830400]{0:T(1024)(128)(4,1)} %bitcast.372), calls=%async_computation.23 | async-start | bytes 8388608
  407.7 120.2 %copy-start.14 = (bf16[960,320]{1,0:T(8,128)(2,1)S(1)}, bf16[960,320]{1,0:T(8,128)(2,1)}, u32[]{:S(2)}) copy-start(bf16[960,320]{1,0:T(8,128)(2,1)} %copy-done.13) | copy-start | bytes 1843204
  407.7 120.2 %copy-start.75 = (bf16[5,64,128]{2,1,0:T(8,128)(2,1)S(1)}, bf16[5,64,128]{2,1,0:T(8,128)(2,1)}, u32[]{:S(2)}) copy-start(bf16[5,64,128]{2,1,0:T(8,128)(2,1)} %fusion.54) | copy-start | bytes 245764
  407.7 120.6 %copy-start.16 = (bf16[960,320]{1,0:T(8,128)(2,1)S(1)}, bf16[960,320]{1,0:T(8,128)(2,1)}, u32[]{:S(2)}) copy-start(bf16[960,320]{1,0:T(8,128)(2,1)} %copy-done.15) | copy-start | bytes 1843204
  515.1 13.6 %copy-start.77 = (bf16[5,64,128]{2,1,0:T(8,128)(2,1)S(1)}, bf16[5,64,128]{2,1,0:T(8,128)(2,1)}, u32[]{:S(2)}) copy-start(bf16[5,64,128]{2,1,0:T(8,128)(2,1)} %fusion.55) | copy-start | bytes 245764
  516.5 96.8 %collective-permute-start.2 = (bf16[32,320]{1,0:T(8,128)(2,1)}, bf16[32,320]{1,0:T(8,128)(2,1)}, u32[]{:S(2)}, u32[]{:S(2)}) collective-permute-start(bf16[32,320]{1,0:T(8,128)(2,1)} %get-tuple-element.50), channel_id=1, source_target_pairs={{0,4},{4,8},{8,12},{12,16},{16,20},{20,24},{24,28},{28,32},{32,36}... | collective-permute-start | bytes 61448
  519.0 100.0 %collective-permute-start.4 = (bf16[32,320]{1,0:T(8,128)(2,1)S(1)}, bf16[32,320]{1,0:T(8,128)(2,1)}, u32[]{:S(2)}, u32[]{:S(2)}) collective-permute-start(bf16[32,320]{1,0:T(8,128)(2,1)S(1)} %get-tuple-element.51), channel_id=1, source_target_pairs={{0,4},{4,8},{8,12},{12,16},{16,20},{20,24},{24,28},{28,32},{32,36}... | collective-permute-start | bytes 61448
  520.9 105.6 %collective-permute-start = (bf16[32,960]{1,0:T(8,128)(2,1)}, bf16[32,960]{1,0:T(8,128)(2,1)}, u32[]{:S(2)}, u32[]{:S(2)}) collective-permute-start(bf16[32,960]{1,0:T(8,128)(2,1)} %get-tuple-element.49), channel_id=1, source_target_pairs={{0,4},{4,8},{8,12},{12,16},{16,20},{20,24},{24,28},{28,32},{32,36}... | collective-permute-start | bytes 184328
  522.9 89.0 %collective-permute-start.3 = (bf16[30,320]{1,0:T(8,128)(2,1)}, bf16[30,320]{1,0:T(8,128)(2,1)}, u32[]{:S(2)}, u32[]{:S(2)}) collective-permute-start(bf16[30,320]{1,0:T(8,128)(2,1)} %slice.187), channel_id=1, source_target_pairs={{0,8},{4,12},{8,16},{12,20},{16,24},{20,28},{24,32},{28,36},{32,40... | collective-permute-start | bytes 57608
  524.8 92.2 %collective-permute-start.5 = (bf16[30,320]{1,0:T(8,128)(2,1)}, bf16[30,320]{1,0:T(8,128)(2,1)}, u32[]{:S(2)}, u32[]{:S(2)}) collective-permute-start(bf16[30,320]{1,0:T(8,128)(2,1)} %slice.188), channel_id=1, source_target_pairs={{0,8},{4,12},{8,16},{12,20},{16,24},{20,28},{24,32},{28,36},{32,40... | collective-permute-start | bytes 57608
  540.9 70.3 %copy-start.60 = (bf16[32,2560]{1,0:T(8,128)(2,1)S(1)}, bf16[32,2560]{1,0:T(8,128)(2,1)}, u32[]{:S(2)}) copy-start(bf16[32,2560]{1,0:T(8,128)(2,1)} %get-tuple-element.53) | copy-start | bytes 491524
  611.9 21.6 %collective-permute-start.6 = (bf16[32,960]{1,0:T(8,128)(2,1)S(1)}, bf16[32,960]{1,0:T(8,128)(2,1)S(1)}, u32[]{:S(2)}, u32[]{:S(2)}) collective-permute-start(bf16[32,960]{1,0:T(8,128)(2,1)S(1)} %get-tuple-element.52), channel_id=1, source_target_pairs={{0,4},{4,8},{8,12},{12,16},{16,20},{20,24},{24,28},{28,32},{32,36}... | collective-permute-start | bytes 184328
  613.2 21.4 %collective-permute-start.8 = (bf16[32,2560]{1,0:T(8,128)(2,1)S(1)}, bf16[32,2560]{1,0:T(8,128)(2,1)S(1)}, u32[]{:S(2)}, u32[]{:S(2)}) collective-permute-start(bf16[32,2560]{1,0:T(8,128)(2,1)S(1)} %copy-done.60), channel_id=1, source_target_pairs={{0,4},{4,8},{8,12},{12,16},{16,20},{20,24},{24,28},{28,32},{32,36}... | collective-permute-start | bytes 491528
  617.0 24.9 %collective-permute-start.10 = (bf16[32,2560]{1,0:T(8,128)(2,1)S(1)}, bf16[32,2560]{1,0:T(8,128)(2,1)}, u32[]{:S(2)}, u32[]{:S(2)}) collective-permute-start(bf16[32,2560]{1,0:T(8,128)(2,1)S(1)} %get-tuple-element.54), channel_id=1, source_target_pairs={{0,4},{4,8},{8,12},{12,16},{16,20},{20,24},{24,28},{28,32},{32,36}... | collective-permute-start | bytes 491528
  619.0 4.4 collective-permute-start.1
  623.4 7.5 %collective-permute-start.7 = (bf16[30,960]{1,0:T(8,128)(2,1)S(1)}, bf16[30,960]{1,0:T(8,128)(2,1)S(1)}, u32[]{:S(2)}, u32[]{:S(2)}) collective-permute-start(bf16[30,960]{1,0:T(8,128)(2,1)S(1)} %slice.189), channel_id=1, source_target_pairs={{0,8},{4,12},{8,16},{12,20},{16,24},{20,28},{24,32},{28,36},{32,40... | collective-permute-start | bytes 172808
  626.4 8.2 %collective-permute-start.9 = (bf16[30,2560]{1,0:T(8,128)(2,1)S(1)}, bf16[30,2560]{1,0:T(8,128)(2,1)S(1)}, u32[]{:S(2)}, u32[]{:S(2)}) collective-permute-start(bf16[30,2560]{1,0:T(8,128)(2,1)S(1)} %slice.190), channel_id=1, source_target_pairs={{0,8},{4,12},{8,16},{12,20},{16,24},{20,28},{24,32},{28,36},{32,40... | collective-permute-start | bytes 460808
  630.9 11.0 %collective-permute-start.11 = (bf16[30,2560]{1,0:T(8,128)(2,1)}, bf16[30,2560]{1,0:T(8,128)(2,1)}, u32[]{:S(2)}, u32[]{:S(2)}) collective-permute-start(bf16[30,2560]{1,0:T(8,128)(2,1)} %slice.191), channel_id=1, source_target_pairs={{0,8},{4,12},{8,16},{12,20},{16,24},{20,28},{24,32},{28,36},{32,40... | collective-permute-start | bytes 460808
  634.6 90.1 %all-reduce.26.cloned.1.call-start = ((), (), s32[]{:S(2)}) async-start(), calls=%async_computation.8 | async-start | bytes 983040 | tf_op jit(solution)/shard_map/psum | solution.py:323
  640.0 12.1 %copy-start.59 = (f32[128,960]{0,1:T(8,128)S(1)}, f32[128,960]{0,1:T(8,128)}, u32[]{:S(2)}) copy-start(f32[128,960]{0,1:T(8,128)} %copy-done.58) | copy-start | bytes 1474564
  640.0 12.1 %copy-start.137 = (f32[128]{0:T(128)S(1)}, f32[128]{0:T(128)}, u32[]{:S(2)}) copy-start(f32[128]{0:T(128)} %get-tuple-element.120) | copy-start | bytes 1540
  640.0 12.1 %copy-start.138 = (f32[128]{0:T(128)S(1)}, f32[128]{0:T(128)}, u32[]{:S(2)}) copy-start(f32[128]{0:T(128)} %get-tuple-element.151) | copy-start | bytes 1540
  640.1 12.1 %copy-start.139 = (f32[128]{0:T(128)S(1)}, f32[128]{0:T(128)}, u32[]{:S(2)}) copy-start(f32[128]{0:T(128)} %get-tuple-element.116) | copy-start | bytes 1540
  640.1 12.1 %copy-start.140 = (f32[128]{0:T(128)S(1)}, f32[128]{0:T(128)}, u32[]{:S(2)}) copy-start(f32[128]{0:T(128)} %broadcast_multiply_fusion.4) | copy-start | bytes 1540
  640.1 12.1 %copy-start.141 = (f32[128]{0:T(128)S(1)}, f32[128]{0:T(128)}, u32[]{:S(2)}) copy-start(f32[128]{0:T(128)} %broadcast_multiply_fusion.2) | copy-start | bytes 1540
  640.1 12.1 %copy-start.142 = (f32[128]{0:T(128)S(1)}, f32[128]{0:T(128)}, u32[]{:S(2)}) copy-start(f32[128]{0:T(128)} %broadcast_multiply_fusion) | copy-start | bytes 1540
  (143 other events, 480.9 us)
Sparse Core Ops, SparseCore 0:
  10.3 46.5 all-gather.13
  59.1 43.2 all-gather.15
  104.7 46.7 all-gather.17
  153.6 46.6 all-gather.19
  202.4 46.8 all-gather.11
  373.9 157.2 reduce-scatter.13
  634.7 44.4 all-reduce.23
  681.8 42.8 all-reduce.25
where the time goes:
time: 748 us; the launch traced here: 737 us
  blocking collectives  289 us (39%)
  matrix products  200 us (27%)
  waiting for transfers between devices  113 us (15%)
  local copies, waits for them, and re-layouts  57.7 us (8%)
  other arithmetic  33.5 us (4%)
  starting transfers between devices  24.7 us (3%)
  between operations  18.2 us (2%)
    unnamed x3, blocking collectives  239 us
    dot_general x21, matrix products, inner_rows(): lax.dot_general(left, right, (((0,), (0,)), ((), ())), preferred_element_...  85.5 us
    unnamed x373, local copies, waits for them, and re-layouts  57.3 us
    dot_general x21, matrix products, times_transposed(): lax.dot_general(left, right, (((1,), (1,)), ((), ())), preferred_element_...  37.9 us
    psum x1, waiting for transfers between devices, local(): lax.psum(s_gate.astype(jnp.bfloat16), 'outer').astype(jnp.float32)  37.4 us
    dot_general x21, matrix products, product(): return jnp.dot(left, right, preferred_element_type=jnp.float32)  37.2 us
    all_gather x1, waiting for transfers between devices, local(): lax.all_gather(w_down, 'dp', axis=0, tiled=True)  34.6 us
    all_gather x1, blocking collectives, local(): lax.all_gather(w_value, 'dp', axis=0, tiled=True)  26.3 us
  transfers between devices with their start and end apart: 20, of which 4 were waited for; matrix products, arithmetic and copies ran while one was open for 36% of the time, Pallas kernels for 0%

commit v1 on v0

v1 whole, which is shorter than its diff:
```python
import math

import jax
import jax.numpy as jnp
from jax import lax
from jax.experimental import pallas as pl
from jax.experimental.pallas import tpu as pltpu
from jax.sharding import PartitionSpec as P

HEADS = 15
KV_HEADS = 5
SHARE = HEADS // KV_HEADS
HEAD_DIM = 64
MB = 128
DOCS = 4
D = 960
FF = 2560
QKV = 1600
ROT = 1280
NX = 4
NZ = 4
PIECES = 32
ROWS = 30
PAD = 32
DP = PIECES * PAD
HALF = DP // 2
DOWN = FF // PIECES

EPSILON = 1e-05
ROPE_BASE = 100000.0
BF = jnp.bfloat16
F32 = jnp.float32


def dot(a, b):
    return jnp.dot(a, b, preferred_element_type=F32)


def dot_nt(a, b):
    return lax.dot_general(a, b, (((1,), (1,)), ((), ())), preferred_element_type=F32)


def dot_tn(a, b):
    return lax.dot_general(a, b, (((0,), (0,)), ((), ())), preferred_element_type=F32)


def rms_scale(v):
    return lax.rsqrt(jnp.mean(v * v, axis=-1, keepdims=True) + EPSILON)


def swap_halves(v):
    n = v.shape[1]
    lane = lax.broadcasted_iota(jnp.int32, v.shape, 1)
    return jnp.where(lane % HEAD_DIM < HEAD_DIM // 2, pltpu.roll(v, n - 32, 1), pltpu.roll(v, 32, 1))


def attn_forward(qkv_ref, cos_ref, sin_ref, segc_ref, segr_ref, rot_ref, out_ref, prob_ref):
    blocks = qkv_ref.shape[0] // MB
    for b in range(blocks):
        rows = slice(b * MB, (b + 1) * MB)
        raw = qkv_ref[rows, :ROT]
        cos = jnp.concatenate([cos_ref[rows, :]] * (ROT // 128), axis=1)
        sin = jnp.concatenate([sin_ref[rows, :]] * (ROT // 128), axis=1)
        rot_ref[rows, :ROT] = (raw * cos + swap_halves(raw) * sin).astype(BF)
        rot_ref[rows, ROT:] = qkv_ref[rows, ROT:].astype(BF)
        r = lax.broadcasted_iota(jnp.int32, (MB, MB), 0)
        t = lax.broadcasted_iota(jnp.int32, (MB, MB), 1)
        allowed = (segc_ref[rows, :] == segr_ref[b : b + 1, :]) & (r >= t)
        allowed = jnp.concatenate([allowed] * SHARE, axis=0)
        for g in range(KV_HEADS):
            q = jnp.concatenate(
                [rot_ref[rows, (g * SHARE + j) * HEAD_DIM : (g * SHARE + j + 1) * HEAD_DIM] for j in range(SHARE)],
                axis=0,
            )
            k = rot_ref[rows, D + g * HEAD_DIM : D + (g + 1) * HEAD_DIM]
            v = rot_ref[rows, ROT + g * HEAD_DIM : ROT + (g + 1) * HEAD_DIM]
            s = jnp.where(allowed, dot_nt(q, k) * HEAD_DIM ** (-0.5), -1e30)
            e = jnp.exp(s - jnp.max(s, axis=-1, keepdims=True))
            p = e / jnp.sum(e, axis=-1, keepdims=True)
            at = (b * KV_HEADS + g) * SHARE * MB
            prob_ref[at : at + SHARE * MB, :] = p
            o = dot(p.astype(BF), v).astype(BF)
            for j in range(SHARE):
                h = g * SHARE + j
                out_ref[rows, h * HEAD_DIM : (h + 1) * HEAD_DIM] = o[j * MB : (j + 1) * MB, :]


def attn_backward(do_ref, rot_ref, prob_ref, cos_ref, sin_ref, dqkv_ref, work_ref):
    blocks = do_ref.shape[0] // MB
    scale = HEAD_DIM ** (-0.5)
    for b in range(blocks):
        rows = slice(b * MB, (b + 1) * MB)
        for g in range(KV_HEADS):
            heads = [slice((g * SHARE + j) * HEAD_DIM, (g * SHARE + j + 1) * HEAD_DIM) for j in range(SHARE)]
            q = jnp.concatenate([rot_ref[rows, h] for h in heads], axis=0)
            do = jnp.concatenate([do_ref[rows, h] for h in heads], axis=0)
            k = rot_ref[rows, D + g * HEAD_DIM : D + (g + 1) * HEAD_DIM]
            v = rot_ref[rows, ROT + g * HEAD_DIM : ROT + (g + 1) * HEAD_DIM]
            at = (b * KV_HEADS + g) * SHARE * MB
            p = prob_ref[at : at + SHARE * MB, :]
            dp = dot_nt(do, v)
            dv = dot_tn(p.astype(BF), do)
            delta = jnp.sum(p * dp, axis=-1, keepdims=True)
            ds = (p * (dp - delta)).astype(BF)
            dq = dot(ds, k) * scale
            dk = dot_tn(ds, q) * scale
            for j in range(SHARE):
                work_ref[:, heads[j]] = dq[j * MB : (j + 1) * MB, :]
            work_ref[:, D + g * HEAD_DIM : D + (g + 1) * HEAD_DIM] = dk
            dqkv_ref[rows, ROT + g * HEAD_DIM : ROT + (g + 1) * HEAD_DIM] = dv.astype(BF)
        cos = jnp.concatenate([cos_ref[rows, :]] * (ROT // 128), axis=1)
        sin = jnp.concatenate([sin_ref[rows, :]] * (ROT // 128), axis=1)
        w = work_ref[...]
        dqkv_ref[rows, :ROT] = (w * cos - swap_halves(w) * sin).astype(BF)


def rope_tables(segment):
    n = segment.shape[0]
    seg = segment.reshape(n // MB, MB)
    index = lax.broadcasted_iota(jnp.int32, (n // MB, MB, MB), 2)
    same = seg[:, :, None] == seg[:, None, :]
    first = jnp.min(jnp.where(same, index, MB), axis=2)
    place = (jnp.arange(MB, dtype=jnp.int32)[None, :] - first).astype(F32).reshape(n, 1)
    lane = jnp.arange(128, dtype=jnp.int32)
    freq = jnp.exp((lane % 32).astype(F32) * (-2.0 * math.log(ROPE_BASE) / HEAD_DIM))
    angles = place * freq[None, :]
    sign = jnp.where(lane % 64 < 32, -1.0, 1.0)[None, :]
    return jnp.cos(angles), jnp.sin(angles) * sign


def padding_matrix(x, z, c):
    i = lax.broadcasted_iota(jnp.int32, (D, HALF), 0)
    j = lax.broadcasted_iota(jnp.int32, (D, HALF), 1)
    j_x = (x + j // (NZ * PAD)) % NX
    j_z = (z + j // PAD % NZ) % NZ
    j_r = j % PAD
    row = ((j_x * NZ + j_z) * 2 + c) * ROWS + j_r
    return ((i == row) & (j_r < ROWS)).astype(BF)


def natural_matrix():
    i = lax.broadcasted_iota(jnp.int32, (D, DP), 0)
    j = lax.broadcasted_iota(jnp.int32, (D, DP), 1)
    return ((i // ROWS) * PAD + i % ROWS == j).astype(BF)


def vmem_call(kernel, out_shape, scratch=()):
    return pl.pallas_call(
        kernel,
        out_shape=out_shape,
        scratch_shapes=list(scratch),
        compiler_params=pltpu.CompilerParams(vmem_limit_bytes=48 * 1024 * 1024),
    )


def place_of(x, z, c):
    return (x * NZ + z) * 2 + c


def shift(v, axis, s):
    perm = []
    for x in range(NX):
        for z in range(NZ):
            for c in range(2):
                to = {
                    "x": ((x + s) % NX, z, c),
                    "z": (x, (z + s) % NZ, c),
                    "c": (x, z, 1 - c),
                }[axis]
                perm.append((place_of(x, z, c), place_of(*to)))
    return lax.ppermute(v, "dp", perm)


def ring_gather(s, axis, cut):
    a = shift(s, axis, 1)
    b = shift(s, axis, -1)
    a2 = shift(a[:cut], axis, 1)
    b2 = shift(b[cut:], axis, -1)
    return [s, b, jnp.concatenate([a2, b2], axis=0), a]


def gather_half(s, first):
    rows, n = s.shape
    second = "z" if first == "x" else "x"
    one = jnp.stack(ring_gather(s, first, rows // 32 * 16), axis=0)
    two = ring_gather(one, second, 2)
    mine = jnp.stack(two, axis=1 if first == "x" else 0)
    return mine, shift(mine, "c", 1)


def ring_sum(take, axis, cut):
    two = take(2)
    from_left = shift(two[:cut], axis, 1)
    from_right = shift(two[cut:], axis, -1)
    one = take(1)
    three = take(3)
    one = jnp.concatenate([one[:cut] + from_left, one[cut:]], axis=0)
    three = jnp.concatenate([three[:cut], three[cut:] + from_right], axis=0)
    a = shift(one, axis, 1)
    b = shift(three, axis, -1)
    return (take(0).astype(F32) + a.astype(F32) + b.astype(F32)).astype(BF)


def reduce_gradient(mine, other, rows, first):
    n = mine.shape[-1]
    h = (mine.astype(F32) + shift(other, "c", 1).astype(F32)).astype(BF).reshape(NX, NZ, rows, n)
    if first == "x":
        h = ring_sum(lambda k: h[k], "x", 2)
        second = "z"
    else:
        h = ring_sum(lambda k: h[:, k], "z", 2)
        second = "x"
    h = ring_sum(lambda k: h[k], second, rows // 32 * 16)
    h = h + lax.ppermute(h, "outer", [(0, 1), (1, 0), (2, 3), (3, 2)])
    t = lax.ppermute(h, "outer", [(0, 3), (3, 0), (1, 2), (2, 1)])
    return h.astype(F32) + t.astype(F32)


def mlp(pos, h2_ref, e_ref, x1_ref, live_ref, wg_ref, wu_ref, dm_ref, do_ref,
        out_ref, dgate_ref, dup_ref, gm_ref, go_ref, dh_ref, acc_ref, w_ref, g_ref):
    step = pl.program_id(0)
    z, c = pos[1], pos[2]

    def at(kz, core):
        return pl.ds(pl.multiple_of(lax.rem(z + kz, NZ) * (2 * DOWN) + core * DOWN, 16), DOWN)

    for kz in range(NZ):
        w_ref[at(kz, c), :] = dm_ref[0, kz]
        w_ref[at(kz, 1 - c), :] = do_ref[0, kz]
    h2 = h2_ref[...]
    e = e_ref[...]
    gate = dot(h2, wg_ref[...])
    up = dot(h2, wu_ref[...])
    sig = jax.nn.sigmoid(gate)
    silu = gate * sig
    hidden = (silu * up).astype(BF)
    g_ref[...] = dot_tn(hidden, e)
    for kz in range(NZ):
        gm_ref[0, kz] = g_ref[at(kz, c), :].astype(BF)
        go_ref[0, kz] = g_ref[at(kz, 1 - c), :].astype(BF)
    d_hidden = dot_nt(e, w_ref[...])
    d_gate = (d_hidden * up * sig * (1.0 + gate * (1.0 - sig))).astype(BF)
    d_up = (d_hidden * silu).astype(BF)
    dgate_ref[...] = d_gate
    dup_ref[...] = d_up
    dh = dot_nt(d_gate, wg_ref[...]) + dot_nt(d_up, wu_ref[...])
    y = dot(hidden, w_ref[...])

    @pl.when(step == 0)
    def _():
        dh_ref[...] = dh
        acc_ref[...] = x1_ref[...] + y

    @pl.when(step > 0)
    def _():
        dh_ref[...] += dh
        acc_ref[...] += y

    @pl.when(step == NX - 1)
    def _():
        out_ref[...] = (acc_ref[...] * live_ref[...]).astype(BF)


def mlp_call(pos, h2, e, x1, live, gate_up, down_mine, down_other):
    n = h2.shape[0]
    tile = FF // NX

    def whole(a):
        return pl.BlockSpec(a.shape, lambda k, pos: (0,) * a.ndim)

    def shard(off):
        return pl.BlockSpec((DP, tile), lambda k, pos: (0, off + lax.rem(pos[0] + k, NX)))

    down = pl.BlockSpec((1, NZ, DOWN, D), lambda k, pos: (k, 0, 0, 0))
    cols = pl.BlockSpec((n, tile), lambda k, pos: (0, lax.rem(pos[0] + k, NX)))
    return pl.pallas_call(
        mlp,
        out_shape=(
            jax.ShapeDtypeStruct((n, D), BF),
            jax.ShapeDtypeStruct((n, FF), BF),
            jax.ShapeDtypeStruct((n, FF), BF),
            jax.ShapeDtypeStruct((NX, NZ, DOWN, D), BF),
            jax.ShapeDtypeStruct((NX, NZ, DOWN, D), BF),
            jax.ShapeDtypeStruct((n, DP), F32),
        ),
        grid_spec=pltpu.PrefetchScalarGridSpec(
            num_scalar_prefetch=1,
            grid=(NX,),
            in_specs=[whole(h2), whole(e), whole(x1), whole(live), shard(0), shard(NX), down, down],
            out_specs=(
                pl.BlockSpec((n, D), lambda k, pos: (0, 0)),
                cols,
                cols,
                down,
                down,
                pl.BlockSpec((n, DP), lambda k, pos: (0, 0)),
            ),
            scratch_shapes=[
                pltpu.VMEM((n, D), F32),
                pltpu.VMEM((tile, D), BF),
                pltpu.VMEM((tile, D), F32),
            ],
        ),
        compiler_params=pltpu.CompilerParams(
            vmem_limit_bytes=48 * 1024 * 1024, dimension_semantics=("arbitrary",)
        ),
        cost_estimate=pl.CostEstimate(flops=14 * n * D * FF, bytes_accessed=30 * 1024 * 1024, transcendentals=n * FF),
    )(pos, h2, e, x1, live, gate_up, gate_up, down_mine, down_other)


def pad_rows(w):
    return jnp.pad(w, ((0, PAD - ROWS), (0, 0)))


def local(
    tokens_in,
    segment_ids,
    norm_in,
    w_query,
    w_key,
    w_value,
    w_out,
    norm_mid,
    w_gate,
    w_up,
    w_down,
    out_cotangent,
):
    n = tokens_in.shape[0]
    me = lax.axis_index("dp")
    c_at = me % 2
    z_at = (me // 2) % NZ
    x_at = me // (2 * NZ)
    pos = jnp.stack([x_at, z_at, c_at]).astype(jnp.int32)
    gain_in = norm_in.astype(F32)[:, None]
    gain_mid = norm_mid.astype(F32)[:, None]
    s_qkv = jnp.concatenate([w_query, w_key, w_value], axis=1).astype(F32)
    s_gu = jnp.concatenate([w_gate, w_up], axis=1).astype(F32)
    gate_up = lax.all_gather(pad_rows((s_gu * gain_mid).astype(BF)), "dp", axis=0, tiled=True)
    qkv_m, qkv_o = gather_half(pad_rows((s_qkv * gain_in).astype(BF)), "x")
    out_m, out_o = gather_half(pad_rows(w_out), "z")
    down_m, down_o = gather_half(w_down, "z")
    qkv_m, qkv_o = qkv_m.reshape(HALF, QKV), qkv_o.reshape(HALF, QKV)
    out_m, out_o = out_m.reshape(HALF, D), out_o.reshape(HALF, D)

    pad_m = padding_matrix(x_at, z_at, c_at)
    pad_o = padding_matrix(x_at, z_at, 1 - c_at)
    natural = natural_matrix()
    cos, sin = rope_tables(segment_ids)
    live = (segment_ids < DOCS).astype(F32)[:, None]
    x = tokens_in.astype(F32)

    s1 = rms_scale(x)
    h1 = (x * s1).astype(BF)
    h1_m, h1_o = dot(h1, pad_m).astype(BF), dot(h1, pad_o).astype(BF)
    qkv = dot(h1_m, qkv_m) + dot(h1_o, qkv_o)
    rot, mixed, probs = vmem_call(
        attn_forward,
        (
            jax.ShapeDtypeStruct((n, QKV), BF),
            jax.ShapeDtypeStruct((n, D), BF),
            jax.ShapeDtypeStruct((n * HEADS, MB), F32),
        ),
    )(qkv, cos, sin, segment_ids[:, None], segment_ids.reshape(n // MB, MB))
    mixed_m, mixed_o = dot(mixed, pad_m).astype(BF), dot(mixed, pad_o).astype(BF)
    x1 = x + dot(mixed_m, out_m) + dot(mixed_o, out_o)
    s2 = rms_scale(x1)
    h2 = (x1 * s2).astype(BF)
    h2_m, h2_o = dot(h2, pad_m).astype(BF), dot(h2, pad_o).astype(BF)
    e_low = (out_cotangent.astype(F32) * live).astype(BF)
    layer_out, d_gate, d_up, gd_m, gd_o, dh2 = mlp_call(
        pos, dot(h2, natural).astype(BF), e_low, x1, live, gate_up, down_m, down_o
    )
    g_down = reduce_gradient(gd_m, gd_o, DOWN, "x")
    d_gu = jnp.concatenate([d_gate, d_up], axis=1)
    g_gu = reduce_gradient(dot_tn(h2_m, d_gu), dot_tn(h2_o, d_gu).astype(BF), PAD, "z")[:ROWS]

    def split(v):
        high = v.astype(BF)
        return high, (v - high.astype(F32)).astype(BF)

    high, low = split(dh2)
    dn = dot_nt(high, natural) + dot_nt(low, natural)
    d_x1 = e_low.astype(F32) + s2 * dn - x1 * s2**3 * jnp.mean(dn * x1, axis=-1, keepdims=True)
    d_a = d_x1.astype(BF)
    d_o = dot_nt(dot_nt(d_a, out_m).astype(BF), pad_m) + dot_nt(dot_nt(d_a, out_o).astype(BF), pad_o)
    d_qkv = vmem_call(
        attn_backward,
        jax.ShapeDtypeStruct((n, QKV), BF),
        [pltpu.VMEM((MB, ROT), F32)],
    )(d_o.astype(BF), rot, probs, cos, sin)

    def att_grad(h1_half, mixed_half):
        return jnp.concatenate([dot_tn(h1_half, d_qkv).astype(BF), dot_tn(mixed_half, d_a).astype(BF)], axis=1)

    g_att = reduce_gradient(att_grad(h1_m, mixed_m), att_grad(h1_o, mixed_o), PAD, "x")[:ROWS]
    dn1 = 0.0
    for w, p in ((qkv_m, pad_m), (qkv_o, pad_o)):
        for part in split(dot_nt(d_qkv, w)):
            dn1 = dn1 + dot_nt(part, p)
    grad_input = (d_x1 + s1 * dn1 - x * s1**3 * jnp.mean(dn1 * x, axis=-1, keepdims=True)).astype(BF)
    g_qkv = g_att[:, :QKV]
    g_norm_in = jnp.sum(g_qkv * s_qkv, axis=1)
    g_norm_mid = jnp.sum(g_gu * s_gu, axis=1)
    g_qkv = g_qkv * gain_in
    g_gu = g_gu * gain_mid
    return (
        layer_out,
        grad_input,
        g_norm_in,
        g_qkv[:, :D],
        g_qkv[:, D:ROT],
        g_qkv[:, ROT:],
        g_att[:, QKV:],
        g_norm_mid,
        g_gu[:, :FF],
        g_gu[:, FF:],
        g_down,
    )


def solution(mesh):
    rows = P(("dp", "outer"), None)
    ids = P(("dp", "outer"))
    vec = P("dp")
    mat = P("dp", None)
    in_specs = (rows, ids, vec, mat, mat, mat, mat, vec, mat, mat, mat, rows)
    out_specs = (rows, rows, vec, mat, mat, mat, mat, vec, mat, mat, mat)
    return jax.shard_map(local, mesh=mesh, in_specs=in_specs, out_specs=out_specs, check_vma=False)
```

time: 748 us -> 402 us (0.54); the launches traced: 737 us -> 398 us
  blocking collectives: 289 us -> 0 us
  matrix products: 200 us -> 48.2 us
  Pallas kernels: 0 us -> 60 us
  starting transfers between devices: 24.7 us -> 83.2 us
  local copies, waits for them, and re-layouts: 57.7 us -> 42.1 us
    unnamed x3 -> x0, blocking collectives: 239 us -> none
    dot_general x78 -> x25, matrix products: 194 us -> 48.2 us  [the longest x6 21.4 us: dot_tn(): lax.dot_general(a, b, (((0,), (0,)), ((), ())), preferred_element_type=F32)]
    ppermute x0 -> x60, waiting for transfers between devices: none -> 118 us  [the longest x54 102 us: shift(): return lax.ppermute(v, 'dp', perm)]
    ppermute x0 -> x60, starting transfers between devices: none -> 83.1 us  [the longest x54 72.9 us: shift(): return lax.ppermute(v, 'dp', perm)]
    psum x2 -> x0, waiting for transfers between devices: 62.1 us -> none  [the longest x1 37.4 us: local(): lax.psum(s_gate.astype(jnp.bfloat16), 'outer').astype(jnp.float32)]
    pallas_call x0 -> x3, Pallas kernels: none -> 60 us  [the longest x1 38.7 us: mlp_call(): pl.pallas_call(mlp, out_shape=(jax.ShapeDtypeStruct((n, D), BF), jax.Shap...]
    all_gather x2 -> x0, blocking collectives: 50.5 us -> none  [the longest x1 26.3 us: local(): lax.all_gather(w_value, 'dp', axis=0, tiled=True)]
    all_gather x5 -> x1, waiting for transfers between devices: 47.5 us -> 0.01 us  [local(): lax.all_gather(pad_rows((s_gu * gain_mid).astype(BF)), 'dp', axis=0, tile...]
  transfers between devices with their start and end apart: 20 -> 61, of which waited for: 4 -> 22; matrix products, arithmetic and copies ran while one was open for 36% -> 22% of each run, Pallas kernels for 0% -> 3%
where the time goes in v1:
time: 402 us; the launch traced here: 398 us
  waiting for transfers between devices  118 us (29%)
  starting transfers between devices  83.2 us (21%)
  Pallas kernels  60 us (15%)
  matrix products  48.2 us (12%)
  local copies, waits for them, and re-layouts  42.1 us (10%)
  other arithmetic  30.5 us (8%)
  between operations  16 us (4%)
    ppermute x54, waiting for transfers between devices, shift(): return lax.ppermute(v, 'dp', perm)  102 us
    ppermute x54, starting transfers between devices, shift(): return lax.ppermute(v, 'dp', perm)  72.9 us
    pallas_call x1, Pallas kernels, mlp_call(): pl.pallas_call(mlp, out_shape=(jax.ShapeDtypeStruct((n, D), BF), jax.Shap...  38.7 us
    dot_general x6, matrix products, dot_tn(): lax.dot_general(a, b, (((0,), (0,)), ((), ())), preferred_element_type=F32)  21.4 us
    dot_general x10, matrix products, dot_nt(): lax.dot_general(a, b, (((1,), (1,)), ((), ())), preferred_element_type=F32)  13.8 us
    unnamed x181, local copies, waits for them, and re-layouts  13 us
    dot_general x9, matrix products, dot(): return jnp.dot(a, b, preferred_element_type=F32)  13 us
    pallas_call x1, Pallas kernels, local(): vmem_call(attn_backward, jax.ShapeDtypeStruct((n, QKV), BF), [pltpu.VMEM(...  11.2 us
  transfers between devices with their start and end apart: 61, of which 22 were waited for; matrix products, arithmetic and copies ran while one was open for 22% of the time, Pallas kernels for 3%

profile of v1, /device:TPU:0, one launch (start us, length us, event | category | flops | bytes accessed | tf_op | source)
XLA Modules:
  0.0 398.2 jit_solution(2112148573177252900)
XLA Ops:
  11.7 2.9 collective-permute-start
  14.6 4.1 %collective-permute-start.9 = (bf16[32,960]{1,0:T(8,128)(2,1)S(1)}, bf16[32,960]{1,0:T(8,128)(2,1)S(1)}, u32[]{:S(2)}, u32[]{:S(2)}) collective-permute-start(bf16[32,960]{1,0:T(8,128)(2,1)S(1)} %get-tuple-element.126), channel_id=1, source_target_pairs={{0,24},{4,28},{8,0},{12,4},{16,8},{20,12},{24,16},{28,20},{32,56},... | collective-permute-start | bytes 184328 | tf_op jit(solution)/shard_map/ppermute | solution.py:171
  22.4 3.3 collective-permute-start.3
  27.7 3.6 collective-permute-done.2
  31.5 3.9 collective-permute-start.4
  35.4 3.3 collective-permute-start.12
  39.5 4.8 %collective-permute-done.4 = bf16[4,32,1600]{2,1,0:T(8,128)(2,1)S(1)} collective-permute-done((bf16[4,32,1600]{2,1,0:T(8,128)(2,1)S(1)}, bf16[4,32,1600]{2,1,0:T(8,128)(2,1)S(1)}, u32[]{:S(2)}, u32[]{:S(2)}) %collective-permute-start.4) | collective-permute-done | bytes 409632 | tf_op jit(solution)/shard_map/ppermute | solution.py:171
  44.4 3.4 collective-permute-start.18
  47.9 2.1 collective-permute-start.6
  52.1 3.7 collective-permute-done.18
  55.8 7.8 %collective-permute-done.7 = bf16[2,32,1600]{2,1,0:T(8,128)(2,1)S(1)} collective-permute-done((bf16[2,32,1600]{2,1,0:T(8,128)(2,1)S(1)}, bf16[2,32,1600]{2,1,0:T(8,128)(2,1)S(1)}, u32[]{:S(2)}, u32[]{:S(2)}) %collective-permute-start.7) | collective-permute-done | bytes 204832 | tf_op jit(solution)/shard_map/ppermute | solution.py:171
  63.6 3.7 collective-permute-start.21
  67.7 3.8 collective-permute-done.21
  78.2 13.9 %collective-permute-done.16 = bf16[2,32,960]{2,1,0:T(8,128)(2,1)S(1)} collective-permute-done((bf16[2,32,960]{2,1,0:T(8,128)(2,1)S(1)}, bf16[2,32,960]{2,1,0:T(8,128)(2,1)S(1)}, u32[]{:S(2)}, u32[]{:S(2)}) %collective-permute-start.16) | collective-permute-done | bytes 122912 | tf_op jit(solution)/shard_map/ppermute | solution.py:171
  98.1 6.9 %collective-permute-done.25 = bf16[2,80,960]{2,1,0:T(8,128)(2,1)S(1)} collective-permute-done((bf16[2,80,960]{2,1,0:T(8,128)(2,1)S(1)}, bf16[2,80,960]{2,1,0:T(8,128)(2,1)S(1)}, u32[]{:S(2)}, u32[]{:S(2)}) %collective-permute-start.25) | collective-permute-done | bytes 307232 | tf_op jit(solution)/shard_map/ppermute | solution.py:171
  110.5 2.5 convolution_add_fusion
  113.0 2.4 copy.117.qkv_ref
  115.4 10.1 %shard_map.203 = (bf16[384,1600]{1,0:T(8,128)(2,1)S(1)}, bf16[384,960]{1,0:T(8,128)(2,1)S(1)}, f32[5760,128]{1,0:T(8,128)}) custom-call(f32[384,1600]{1,0:T(8,128)S(1)} %copy.117.qkv_ref, f32[384,128]{1,0:T(8,128)S(1)} %get-tuple-element.128.cos_ref, f32[384,128]{1,0:T(8,128)S(1)} %get-tuple-element.127.sin_ref, s32[384,1]{1,0:T(8,128)S(1)} %broadcast_in_dim.32.segc_ref, ...), custom_call_target="tpu_custom_call" | custom-call | tf_op jit(solution)/shard_map/pallas_call | solution.py:357
  133.2 2.4 convolution_convert_fusion.5.h2_ref
  136.8 38.7 %shard_map.204 = (bf16[384,960]{1,0:T(8,128)(2,1)S(1)}, bf16[384,2560]{1,0:T(8,128)(2,1)}, bf16[384,2560]{1,0:T(8,128)(2,1)}, bf16[4,4,80,960]{3,2,1,0:T(8,128)(...) custom-call(s32[3]{0:T(128)S(1)} %pad_add_fusion.pos, bf16[384,1024]{1,0:T(8,128)(2,1)S(1)} %copy-done.8, ...), custom_call_target="tpu_custom_call" | custom-call | flops 13212057600 | bytes 31457280 | tf_op jit(solution)/shard_map/pallas_call | solution.py:276
  180.4 2.5 fusion.22
  182.8 3.4 convolution_add_fusion.2
  187.7 11.2 %shard_map.205 = bf16[384,1600]{1,0:T(8,128)(2,1)S(1)} custom-call(bf16[384,960]{1,0:T(8,128)(2,1)S(1)} %copy.125.do_ref, bf16[384,1600]{1,0:T(8,128)(2,1)S(1)} %copy-done.1, f32[5760,128]{1,0:T(8,128)} %get-tuple-element.24.prob_ref, f32[384,128]{1,0:T(8,128)S(1)} %get-tuple-element.128.cos_ref, f32[384,128]{1,0:T(8,128)S(1)} %get-tuple-element.127.sin_ref), custom_call_target="tpu_custom_call" | custom-call | tf_op jit(solution)/shard_map/pallas_call | solution.py:387
  216.9 8.4 %convolution_convert_fusion = bf16[512,5120]{1,0:T(8,128)(2,1)} fusion(bf16[384,5120]{1,0:T(8,128)(2,1)} %copy-done.34, bf16[384,960]{1,0:T(8,128)(2,1)S(1)} %copy-done.38, s32[]{:T(128)S(6)} %sub.69, s32[512]{0:T(512)S(1)} %copy-done.62, s32[512]{0:T(512)S(1)} %copy-done.65, pred[512]{0:T(512)(128)(4,1)} %copy-done.82, s32[512]{0:T(512)} %copy-done.70, ...), kind=kOutput, calls=%fused_computation.1 | convolution fusion | flops 2416672768 | bytes 9926156 | tf_op jit(solution)/shard_map/dot_general | solution.py:44
  228.6 3.0 add_convert_fusion.1
  232.7 3.2 collective-permute-start.52
  235.9 2.5 add_convert_fusion.2
  238.4 2.4 fusion.92
  241.9 2.8 copy.130
  261.4 6.6 %collective-permute-done.28 = bf16[2,32,2560]{2,1,0:T(8,128)(2,1)S(1)} collective-permute-done((bf16[2,32,2560]{2,1,0:T(8,128)(2,1)}, bf16[2,32,2560]{2,1,0:T(8,128)(2,1)S(1)}, u32[]{:S(2)}, u32[]{:S(2)}) %collective-permute-start.28) | collective-permute-done | bytes 327712 | tf_op jit(solution)/shard_map/ppermute | solution.py:171
  270.8 2.5 collective-permute-start.31
  273.3 7.4 %collective-permute-done.53 = bf16[4,80,960]{2,1,0:T(8,128)(2,1)S(1)} collective-permute-done((bf16[4,80,960]{2,1,0:T(8,128)(2,1)S(1)}, bf16[4,80,960]{2,1,0:T(8,128)(2,1)S(1)}, u32[]{:S(2)}, u32[]{:S(2)}) %collective-permute-start.53) | collective-permute-done | bytes 614432 | tf_op jit(solution)/shard_map/ppermute | solution.py:171
  285.8 2.2 collective-permute-done.54
  288.9 3.0 collective-permute-start.57
  292.0 9.4 %add_convert_fusion = bf16[512,5120]{1,0:T(8,128)(2,1)} fusion(bf16[512,5120]{1,0:T(8,128)(2,1)} %collective-permute-done.38, bf16[384,5120]{1,0:T(8,128)(2,1)} %copy-done.34, bf16[384,960]{1,0:T(8,128)(2,1)} %copy-done.37, s32[512]{0:T(512)S(1)} %copy-done.62, s32[512]{0:T(512)S(1)} %copy-done.66, s32[]{:T(128)} %select_n.112, ...), kind=kOutput, calls=%fused_computation | convolution fusion | flops 2421915648 | bytes 15169036 | tf_op jit(solution)/shard_map/dot_general | solution.py:44
  303.4 3.2 collective-permute-start.41
  308.2 9.5 %collective-permute-done.39 = bf16[2,32,5120]{2,1,0:T(8,128)(2,1)S(1)} collective-permute-done((bf16[2,32,5120]{2,1,0:T(8,128)(2,1)S(1)}, bf16[2,32,5120]{2,1,0:T(8,128)(2,1)S(1)}, u32[]{:S(2)}, u32[]{:S(2)}) %collective-permute-start.39) | collective-permute-done | bytes 655392 | tf_op jit(solution)/shard_map/ppermute | solution.py:171
  317.9 3.6 collective-permute-start.42
  321.9 3.3 collective-permute-start.34
  326.8 22.9 %collective-permute-done.32 = bf16[16,2560]{1,0:T(8,128)(2,1)S(1)} collective-permute-done((bf16[16,2560]{1,0:T(8,128)(2,1)S(1)}, bf16[16,2560]{1,0:T(8,128)(2,1)S(1)}, u32[]{:S(2)}, u32[]{:S(2)}) %collective-permute-start.32) | collective-permute-done | bytes 81952 | tf_op jit(solution)/shard_map/ppermute | solution.py:171
  349.7 2.5 collective-permute-start.35
  353.0 3.2 collective-permute-start.45
  356.4 2.8 collective-permute-start.59
  359.2 2.1 collective-permute-done.43
  365.9 4.9 %collective-permute-done.36 = bf16[32,2560]{1,0:T(8,128)(2,1)S(1)} collective-permute-done((bf16[32,2560]{1,0:T(8,128)(2,1)S(1)}, bf16[32,2560]{1,0:T(8,128)(2,1)S(1)}, u32[]{:S(2)}, u32[]{:S(2)}) %collective-permute-start.36) | collective-permute-done | bytes 163872 | tf_op jit(solution)/shard_map/ppermute | solution.py:214
  370.9 2.8 collective-permute-start.37
  374.2 5.1 %collective-permute-done.37 = bf16[32,2560]{1,0:T(8,128)(2,1)S(1)} collective-permute-done((bf16[32,2560]{1,0:T(8,128)(2,1)S(1)}, bf16[32,2560]{1,0:T(8,128)(2,1)S(1)}, u32[]{:S(2)}, u32[]{:S(2)}) %collective-permute-start.37) | collective-permute-done | bytes 163872 | tf_op jit(solution)/shard_map/ppermute | solution.py:215
  385.0 4.5 %collective-permute-done.48 = bf16[32,5120]{1,0:T(8,128)(2,1)S(1)} collective-permute-done((bf16[32,5120]{1,0:T(8,128)(2,1)S(1)}, bf16[32,5120]{1,0:T(8,128)(2,1)S(1)}, u32[]{:S(2)}, u32[]{:S(2)}) %collective-permute-start.48) | collective-permute-done | bytes 327712 | tf_op jit(solution)/shard_map/ppermute | solution.py:215
  (401 shorter events, 114.1 us)
Async XLA Ops:
  7.2 128.4 %all-gather.2.cloned.1.call-start = ((), (), s32[]{:S(2)}) async-start(), calls=%async_computation | async-start | bytes 10813440 | tf_op jit(solution)/shard_map/all_gather | solution.py:339
  11.7 10.7 %collective-permute-start = (bf16[32,1600]{1,0:T(8,128)(2,1)S(1)}, bf16[32,1600]{1,0:T(8,128)(2,1)S(1)}, u32[]{:S(2)}, u32[]{:S(2)}) collective-permute-start(bf16[32,1600]{1,0:T(8,128)(2,1)S(1)} %get-tuple-element.124), channel_id=1, source_target_pairs={{0,96},{4,100},{8,104},{12,108},{16,112},{20,116},{24,120},{28,124... | collective-permute-start | bytes 307208 | tf_op jit(solution)/shard_map/ppermute | solution.py:171
  14.6 11.1 %collective-permute-start.1 = (bf16[32,1600]{1,0:T(8,128)(2,1)S(1)}, bf16[32,1600]{1,0:T(8,128)(2,1)S(1)}, u32[]{:S(2)}, u32[]{:S(2)}) collective-permute-start(bf16[32,1600]{1,0:T(8,128)(2,1)S(1)} %get-tuple-element.124), channel_id=1, source_target_pairs={{0,32},{4,36},{8,40},{12,44},{16,48},{20,52},{24,56},{28,60},{32,6... | collective-permute-start | bytes 307208 | tf_op jit(solution)/shard_map/ppermute | solution.py:171
  14.6 20.8 %collective-permute-start.9 = (bf16[32,960]{1,0:T(8,128)(2,1)S(1)}, bf16[32,960]{1,0:T(8,128)(2,1)S(1)}, u32[]{:S(2)}, u32[]{:S(2)}) collective-permute-start(bf16[32,960]{1,0:T(8,128)(2,1)S(1)} %get-tuple-element.126), channel_id=1, source_target_pairs={{0,24},{4,28},{8,0},{12,4},{16,8},{20,12},{24,16},{28,20},{32,56},... | collective-permute-start | bytes 184328 | tf_op jit(solution)/shard_map/ppermute | solution.py:171
  18.7 20.0 %collective-permute-start.10 = (bf16[32,960]{1,0:T(8,128)(2,1)S(1)}, bf16[32,960]{1,0:T(8,128)(2,1)S(1)}, u32[]{:S(2)}, u32[]{:S(2)}) collective-permute-start(bf16[32,960]{1,0:T(8,128)(2,1)S(1)} %get-tuple-element.126), channel_id=1, source_target_pairs={{0,8},{4,12},{8,16},{12,20},{16,24},{20,28},{24,0},{28,4},{32,40},... | collective-permute-start | bytes 184328 | tf_op jit(solution)/shard_map/ppermute | solution.py:171
  18.7 32.3 %collective-permute-start.19 = (bf16[80,960]{1,0:T(8,128)(2,1)S(1)}, bf16[80,960]{1,0:T(8,128)(2,1)S(1)}, u32[]{:S(2)}, u32[]{:S(2)}) collective-permute-start(bf16[80,960]{1,0:T(8,128)(2,1)S(1)} %copy-done.47), channel_id=1, source_target_pairs={{0,8},{4,12},{8,16},{12,20},{16,24},{20,28},{24,0},{28,4},{32,40},... | collective-permute-start | bytes 460808 | tf_op jit(solution)/shard_map/ppermute | solution.py:171
  31.5 12.9 %collective-permute-start.4 = (bf16[4,32,1600]{2,1,0:T(8,128)(2,1)S(1)}, bf16[4,32,1600]{2,1,0:T(8,128)(2,1)S(1)}, u32[]{:S(2)}, u32[]{:S(2)}) collective-permute-start(bf16[4,32,1600]{2,1,0:T(8,128)(2,1)S(1)} %get-tuple-element.116), channel_id=1, source_target_pairs={{0,24},{4,28},{8,0},{12,4},{16,8},{20,12},{24,16},{28,20},{32,56},... | collective-permute-start | bytes 1228808 | tf_op jit(solution)/shard_map/ppermute | solution.py:171
  35.4 12.4 %collective-permute-start.5 = (bf16[4,32,1600]{2,1,0:T(8,128)(2,1)S(1)}, bf16[4,32,1600]{2,1,0:T(8,128)(2,1)S(1)}, u32[]{:S(2)}, u32[]{:S(2)}) collective-permute-start(bf16[4,32,1600]{2,1,0:T(8,128)(2,1)S(1)} %get-tuple-element.116), channel_id=1, source_target_pairs={{0,8},{4,12},{8,16},{12,20},{16,24},{20,28},{24,0},{28,4},{32,40},... | collective-permute-start | bytes 1228808 | tf_op jit(solution)/shard_map/ppermute | solution.py:171
  35.4 12.4 %collective-permute-start.12 = (bf16[16,960]{1,0:T(8,128)(2,1)S(1)}, bf16[16,960]{1,0:T(8,128)(2,1)S(1)}, u32[]{:S(2)}, u32[]{:S(2)}) collective-permute-start(bf16[16,960]{1,0:T(8,128)(2,1)S(1)} %slice.458), channel_id=1, source_target_pairs={{0,24},{4,28},{8,0},{12,4},{16,8},{20,12},{24,16},{28,20},{32,56},... | collective-permute-start | bytes 92168 | tf_op jit(solution)/shard_map/ppermute | solution.py:171
  38.7 11.2 %collective-permute-start.11 = (bf16[16,960]{1,0:T(8,128)(2,1)S(1)}, bf16[16,960]{1,0:T(8,128)(2,1)S(1)}, u32[]{:S(2)}, u32[]{:S(2)}) collective-permute-start(bf16[16,960]{1,0:T(8,128)(2,1)S(1)} %slice.457), channel_id=1, source_target_pairs={{0,8},{4,12},{8,16},{12,20},{16,24},{20,28},{24,0},{28,4},{32,40},... | collective-permute-start | bytes 92168 | tf_op jit(solution)/shard_map/ppermute | solution.py:171
  44.4 11.4 %collective-permute-start.18 = (bf16[80,960]{1,0:T(8,128)(2,1)S(1)}, bf16[80,960]{1,0:T(8,128)(2,1)S(1)}, u32[]{:S(2)}, u32[]{:S(2)}) collective-permute-start(bf16[80,960]{1,0:T(8,128)(2,1)S(1)} %copy-done.47), channel_id=1, source_target_pairs={{0,24},{4,28},{8,0},{12,4},{16,8},{20,12},{24,16},{28,20},{32,56},... | collective-permute-start | bytes 460808 | tf_op jit(solution)/shard_map/ppermute | solution.py:171
  47.8 15.8 %collective-permute-start.7 = (bf16[2,32,1600]{2,1,0:T(8,128)(2,1)S(1)}, bf16[2,32,1600]{2,1,0:T(8,128)(2,1)S(1)}, u32[]{:S(2)}, u32[]{:S(2)}) collective-permute-start(bf16[2,32,1600]{2,1,0:T(8,128)(2,1)S(1)} %slice.456), channel_id=1, source_target_pairs={{0,24},{4,28},{8,0},{12,4},{16,8},{20,12},{24,16},{28,20},{32,56},... | collective-permute-start | bytes 614408 | tf_op jit(solution)/shard_map/ppermute | solution.py:171
  47.9 19.4 %collective-permute-start.6 = (bf16[2,32,1600]{2,1,0:T(8,128)(2,1)S(1)}, bf16[2,32,1600]{2,1,0:T(8,128)(2,1)S(1)}, u32[]{:S(2)}, u32[]{:S(2)}) collective-permute-start(bf16[2,32,1600]{2,1,0:T(8,128)(2,1)S(1)} %slice.455), channel_id=1, source_target_pairs={{0,8},{4,12},{8,16},{12,20},{16,24},{20,28},{24,0},{28,4},{32,40},... | collective-permute-start | bytes 614408 | tf_op jit(solution)/shard_map/ppermute | solution.py:171
  50.0 25.1 %collective-permute-start.13 = (bf16[4,32,960]{2,1,0:T(8,128)(2,1)S(1)}, bf16[4,32,960]{2,1,0:T(8,128)(2,1)S(1)}, u32[]{:S(2)}, u32[]{:S(2)}) collective-permute-start(bf16[4,32,960]{2,1,0:T(8,128)(2,1)S(1)} %get-tuple-element.120), channel_id=1, source_target_pairs={{0,96},{4,100},{8,104},{12,108},{16,112},{20,116},{24,120},{28,124... | collective-permute-start | bytes 737288 | tf_op jit(solution)/shard_map/ppermute | solution.py:171
  51.0 26.2 %collective-permute-start.14 = (bf16[4,32,960]{2,1,0:T(8,128)(2,1)S(1)}, bf16[4,32,960]{2,1,0:T(8,128)(2,1)S(1)}, u32[]{:S(2)}, u32[]{:S(2)}) collective-permute-start(bf16[4,32,960]{2,1,0:T(8,128)(2,1)S(1)} %get-tuple-element.120), channel_id=1, source_target_pairs={{0,32},{4,36},{8,40},{12,44},{16,48},{20,52},{24,56},{28,60},{32,6... | collective-permute-start | bytes 737288 | tf_op jit(solution)/shard_map/ppermute | solution.py:171
  55.8 11.9 %collective-permute-start.20 = (bf16[32,960]{1,0:T(8,128)(2,1)S(1)}, bf16[32,960]{1,0:T(8,128)(2,1)S(1)}, u32[]{:S(2)}, u32[]{:S(2)}) collective-permute-start(bf16[32,960]{1,0:T(8,128)(2,1)S(1)} %slice.461), channel_id=1, source_target_pairs={{0,8},{4,12},{8,16},{12,20},{16,24},{20,28},{24,0},{28,4},{32,40},... | collective-permute-start | bytes 184328 | tf_op jit(solution)/shard_map/ppermute | solution.py:171
  67.6 41.5 %collective-permute-start.8 = (bf16[4,4,32,1600]{3,2,0,1:T(8,128)(2,1)S(1)}, bf16[4,4,32,1600]{3,2,0,1:T(8,128)(2,1)S(1)}, u32[]{:S(2)}, u32[]{:S(2)}) collective-permute-start(bf16[4,4,32,1600]{3,2,0,1:T(8,128)(2,1)S(1)} %pad_maximum_fusion.2), channel_id=1, source_target_pairs={{0,4},{4,0},{8,12},{12,8},{16,20},{20,16},{24,28},{28,24},{32,36},... | collective-permute-start | bytes 4915208 | tf_op jit(solution)/shard_map/ppermute | solution.py:171
  71.6 23.2 %collective-permute-start.22 = (bf16[4,80,960]{2,1,0:T(8,128)(2,1)S(1)}, bf16[4,80,960]{2,1,0:T(8,128)(2,1)S(1)}, u32[]{:S(2)}, u32[]{:S(2)}) collective-permute-start(bf16[4,80,960]{2,1,0:T(8,128)(2,1)S(1)} %get-tuple-element.114), channel_id=1, source_target_pairs={{0,96},{4,100},{8,104},{12,108},{16,112},{20,116},{24,120},{28,124... | collective-permute-start | bytes 1843208 | tf_op jit(solution)/shard_map/ppermute | solution.py:171
  72.7 23.0 %collective-permute-start.23 = (bf16[4,80,960]{2,1,0:T(8,128)(2,1)S(1)}, bf16[4,80,960]{2,1,0:T(8,128)(2,1)S(1)}, u32[]{:S(2)}, u32[]{:S(2)}) collective-permute-start(bf16[4,80,960]{2,1,0:T(8,128)(2,1)S(1)} %get-tuple-element.114), channel_id=1, source_target_pairs={{0,32},{4,36},{8,40},{12,44},{16,48},{20,52},{24,56},{28,60},{32,6... | collective-permute-start | bytes 1843208 | tf_op jit(solution)/shard_map/ppermute | solution.py:171
  75.1 17.0 %collective-permute-start.16 = (bf16[2,32,960]{2,1,0:T(8,128)(2,1)S(1)}, bf16[2,32,960]{2,1,0:T(8,128)(2,1)S(1)}, u32[]{:S(2)}, u32[]{:S(2)}) collective-permute-start(bf16[2,32,960]{2,1,0:T(8,128)(2,1)S(1)} %slice.460), channel_id=1, source_target_pairs={{0,96},{4,100},{8,104},{12,108},{16,112},{20,116},{24,120},{28,124... | collective-permute-start | bytes 368648 | tf_op jit(solution)/shard_map/ppermute | solution.py:171
  77.2 16.3 %collective-permute-start.15 = (bf16[2,32,960]{2,1,0:T(8,128)(2,1)S(1)}, bf16[2,32,960]{2,1,0:T(8,128)(2,1)S(1)}, u32[]{:S(2)}, u32[]{:S(2)}) collective-permute-start(bf16[2,32,960]{2,1,0:T(8,128)(2,1)S(1)} %slice.459), channel_id=1, source_target_pairs={{0,32},{4,36},{8,40},{12,44},{16,48},{20,52},{24,56},{28,60},{32,6... | collective-permute-start | bytes 368648 | tf_op jit(solution)/shard_map/ppermute | solution.py:171
  94.6 35.6 %collective-permute-start.17 = (bf16[4,4,32,960]{3,2,1,0:T(8,128)(2,1)}, bf16[4,4,32,960]{3,2,1,0:T(8,128)(2,1)}, u32[]{:S(2)}, u32[]{:S(2)}) collective-permute-start(bf16[4,4,32,960]{3,2,1,0:T(8,128)(2,1)} %pad_maximum_fusion.5), channel_id=1, source_target_pairs={{0,4},{4,0},{8,12},{12,8},{16,20},{20,16},{24,28},{28,24},{32,36},... | collective-permute-start | bytes 2949128 | tf_op jit(solution)/shard_map/ppermute | solution.py:171
  94.8 10.2 %collective-permute-start.25 = (bf16[2,80,960]{2,1,0:T(8,128)(2,1)S(1)}, bf16[2,80,960]{2,1,0:T(8,128)(2,1)S(1)}, u32[]{:S(2)}, u32[]{:S(2)}) collective-permute-start(bf16[2,80,960]{2,1,0:T(8,128)(2,1)S(1)} %slice.464), channel_id=1, source_target_pairs={{0,96},{4,100},{8,104},{12,108},{16,112},{20,116},{24,120},{28,124... | collective-permute-start | bytes 921608 | tf_op jit(solution)/shard_map/ppermute | solution.py:171
  95.7 11.1 %collective-permute-start.24 = (bf16[2,80,960]{2,1,0:T(8,128)(2,1)S(1)}, bf16[2,80,960]{2,1,0:T(8,128)(2,1)S(1)}, u32[]{:S(2)}, u32[]{:S(2)}) collective-permute-start(bf16[2,80,960]{2,1,0:T(8,128)(2,1)S(1)} %slice.463), channel_id=1, source_target_pairs={{0,32},{4,36},{8,40},{12,44},{16,48},{20,52},{24,56},{28,60},{32,6... | collective-permute-start | bytes 921608 | tf_op jit(solution)/shard_map/ppermute | solution.py:171
  108.8 26.8 %collective-permute-start.26 = (bf16[4,4,80,960]{3,2,1,0:T(8,128)(2,1)}, bf16[4,4,80,960]{3,2,1,0:T(8,128)(2,1)}, u32[]{:S(2)}, u32[]{:S(2)}) collective-permute-start(bf16[4,4,80,960]{3,2,1,0:T(8,128)(2,1)} %pad_maximum_fusion.dm_ref), channel_id=1, source_target_pairs={{0,4},{4,0},{8,12},{12,8},{16,20},{20,16},{24,28},{28,24},{32,36},... | collective-permute-start | bytes 7372808 | tf_op jit(solution)/shard_map/ppermute | solution.py:171
  209.2 26.7 %collective-permute-start.27 = (bf16[512,2560]{0,1:T(8,128)(2,1)}, bf16[512,2560]{0,1:T(8,128)(2,1)}, u32[]{:S(2)}, u32[]{:S(2)}) collective-permute-start(bf16[512,2560]{0,1:T(8,128)(2,1)} %pad_maximum_fusion.1), channel_id=1, source_target_pairs={{0,4},{4,0},{8,12},{12,8},{16,20},{20,16},{24,28},{28,24},{32,36},... | collective-permute-start | bytes 7864328 | tf_op jit(solution)/shard_map/ppermute | solution.py:171
  209.7 18.2 %collective-permute-start.49 = (bf16[4,4,80,960]{3,2,1,0:T(8,128)(2,1)}, bf16[4,4,80,960]{3,2,1,0:T(8,128)(2,1)}, u32[]{:S(2)}, u32[]{:S(2)}) collective-permute-start(bf16[4,4,80,960]{3,2,1,0:T(8,128)(2,1)} %get-tuple-element.28), channel_id=1, source_target_pairs={{0,4},{4,0},{8,12},{12,8},{16,20},{20,16},{24,28},{28,24},{32,36},... | collective-permute-start | bytes 7372808 | tf_op jit(solution)/shard_map/ppermute | solution.py:171
  225.3 66.6 %collective-permute-start.38 = (bf16[512,5120]{1,0:T(8,128)(2,1)}, bf16[512,5120]{1,0:T(8,128)(2,1)}, u32[]{:S(2)}, u32[]{:S(2)}) collective-permute-start(bf16[512,5120]{1,0:T(8,128)(2,1)} %convolution_convert_fusion), channel_id=1, source_target_pairs={{0,4},{4,0},{8,12},{12,8},{16,20},{20,16},{24,28},{28,24},{32,36},... | collective-permute-start | bytes 15728648 | tf_op jit(solution)/shard_map/ppermute | solution.py:171
  232.7 25.2 %collective-permute-start.50 = (bf16[2,80,960]{2,1,0:T(8,128)(2,1)}, bf16[2,80,960]{2,1,0:T(8,128)(2,1)}, u32[]{:S(2)}, u32[]{:S(2)}) collective-permute-start(bf16[2,80,960]{2,1,0:T(8,128)(2,1)} %get-tuple-element.83), channel_id=1, source_target_pairs={{0,32},{4,36},{8,40},{12,44},{16,48},{20,52},{24,56},{28,60},{32,6... | collective-permute-start | bytes 921608 | tf_op jit(solution)/shard_map/ppermute | solution.py:171
  232.7 25.2 %collective-permute-start.52 = (bf16[2,80,960]{2,1,0:T(8,128)(2,1)}, bf16[2,80,960]{2,1,0:T(8,128)(2,1)}, u32[]{:S(2)}, u32[]{:S(2)}) collective-permute-start(bf16[2,80,960]{2,1,0:T(8,128)(2,1)} %get-tuple-element.84), channel_id=1, source_target_pairs={{0,96},{4,100},{8,104},{12,108},{16,112},{20,116},{24,120},{28,124... | collective-permute-start | bytes 921608 | tf_op jit(solution)/shard_map/ppermute | solution.py:171
  255.9 13.9 %collective-permute-start.30 = (bf16[2,32,2560]{2,1,0:T(8,128)(2,1)}, bf16[2,32,2560]{2,1,0:T(8,128)(2,1)S(1)}, u32[]{:S(2)}, u32[]{:S(2)}) collective-permute-start(bf16[2,32,2560]{2,1,0:T(8,128)(2,1)} %bitcast.224), channel_id=1, source_target_pairs={{0,96},{4,100},{8,104},{12,108},{16,112},{20,116},{24,120},{28,124... | collective-permute-start | bytes 983048 | tf_op jit(solution)/shard_map/ppermute | solution.py:171
  255.9 12.1 %collective-permute-start.28 = (bf16[2,32,2560]{2,1,0:T(8,128)(2,1)}, bf16[2,32,2560]{2,1,0:T(8,128)(2,1)S(1)}, u32[]{:S(2)}, u32[]{:S(2)}) collective-permute-start(bf16[2,32,2560]{2,1,0:T(8,128)(2,1)} %bitcast.225), channel_id=1, source_target_pairs={{0,32},{4,36},{8,40},{12,44},{16,48},{20,52},{24,56},{28,60},{32,6... | collective-permute-start | bytes 983048 | tf_op jit(solution)/shard_map/ppermute | solution.py:171
  259.1 21.6 %collective-permute-start.53 = (bf16[4,80,960]{2,1,0:T(8,128)(2,1)S(1)}, bf16[4,80,960]{2,1,0:T(8,128)(2,1)S(1)}, u32[]{:S(2)}, u32[]{:S(2)}) collective-permute-start(bf16[4,80,960]{2,1,0:T(8,128)(2,1)S(1)} %pad_maximum_fusion.10), channel_id=1, source_target_pairs={{0,96},{4,100},{8,104},{12,108},{16,112},{20,116},{24,120},{28,124... | collective-permute-start | bytes 1843208 | tf_op jit(solution)/shard_map/ppermute | solution.py:171
  260.6 21.4 %collective-permute-start.51 = (bf16[4,80,960]{2,1,0:T(8,128)(2,1)S(1)}, bf16[4,80,960]{2,1,0:T(8,128)(2,1)S(1)}, u32[]{:S(2)}, u32[]{:S(2)}) collective-permute-start(bf16[4,80,960]{2,1,0:T(8,128)(2,1)S(1)} %pad_maximum_fusion.9), channel_id=1, source_target_pairs={{0,32},{4,36},{8,40},{12,44},{16,48},{20,52},{24,56},{28,60},{32,6... | collective-permute-start | bytes 1843208 | tf_op jit(solution)/shard_map/ppermute | solution.py:171
  269.0 34.5 %collective-permute-start.29 = (bf16[4,32,2560]{2,1,0:T(8,128)(2,1)}, bf16[4,32,2560]{2,1,0:T(8,128)(2,1)}, u32[]{:S(2)}, u32[]{:S(2)}) collective-permute-start(bf16[4,32,2560]{2,1,0:T(8,128)(2,1)} %pad_maximum_fusion.7), channel_id=1, source_target_pairs={{0,32},{4,36},{8,40},{12,44},{16,48},{20,52},{24,56},{28,60},{32,6... | collective-permute-start | bytes 1966088 | tf_op jit(solution)/shard_map/ppermute | solution.py:171
  270.8 35.9 %collective-permute-start.31 = (bf16[4,32,2560]{2,1,0:T(8,128)(2,1)}, bf16[4,32,2560]{2,1,0:T(8,128)(2,1)}, u32[]{:S(2)}, u32[]{:S(2)}) collective-permute-start(bf16[4,32,2560]{2,1,0:T(8,128)(2,1)} %pad_maximum_fusion.8), channel_id=1, source_target_pairs={{0,96},{4,100},{8,104},{12,108},{16,112},{20,116},{24,120},{28,124... | collective-permute-start | bytes 1966088 | tf_op jit(solution)/shard_map/ppermute | solution.py:171
  288.0 33.9 %collective-permute-start.55 = (bf16[80,960]{1,0:T(8,128)(2,1)S(1)}, bf16[80,960]{1,0:T(8,128)(2,1)S(1)}, u32[]{:S(2)}, u32[]{:S(2)}) collective-permute-start(bf16[80,960]{1,0:T(8,128)(2,1)S(1)} %pad_maximum_fusion.18), channel_id=1, source_target_pairs={{0,8},{4,12},{8,16},{12,20},{16,24},{20,28},{24,0},{28,4},{32,40},... | collective-permute-start | bytes 460808 | tf_op jit(solution)/shard_map/ppermute | solution.py:171
  288.9 36.2 %collective-permute-start.57 = (bf16[80,960]{1,0:T(8,128)(2,1)S(1)}, bf16[80,960]{1,0:T(8,128)(2,1)S(1)}, u32[]{:S(2)}, u32[]{:S(2)}) collective-permute-start(bf16[80,960]{1,0:T(8,128)(2,1)S(1)} %pad_maximum_fusion.19), channel_id=1, source_target_pairs={{0,24},{4,28},{8,0},{12,4},{16,8},{20,12},{24,16},{28,20},{32,56},... | collective-permute-start | bytes 460808 | tf_op jit(solution)/shard_map/ppermute | solution.py:171
  303.3 14.3 %collective-permute-start.39 = (bf16[2,32,5120]{2,1,0:T(8,128)(2,1)S(1)}, bf16[2,32,5120]{2,1,0:T(8,128)(2,1)S(1)}, u32[]{:S(2)}, u32[]{:S(2)}) collective-permute-start(bf16[2,32,5120]{2,1,0:T(8,128)(2,1)S(1)} %get-tuple-element.77), channel_id=1, source_target_pairs={{0,8},{4,12},{8,16},{12,20},{16,24},{20,28},{24,0},{28,4},{32,40},... | collective-permute-start | bytes 1966088 | tf_op jit(solution)/shard_map/ppermute | solution.py:171
  303.4 14.2 %collective-permute-start.41 = (bf16[2,32,5120]{2,1,0:T(8,128)(2,1)S(1)}, bf16[2,32,5120]{2,1,0:T(8,128)(2,1)S(1)}, u32[]{:S(2)}, u32[]{:S(2)}) collective-permute-start(bf16[2,32,5120]{2,1,0:T(8,128)(2,1)S(1)} %get-tuple-element.80), channel_id=1, source_target_pairs={{0,24},{4,28},{8,0},{12,4},{16,8},{20,12},{24,16},{28,20},{32,56},... | collective-permute-start | bytes 1966088 | tf_op jit(solution)/shard_map/ppermute | solution.py:171
  317.9 34.3 %collective-permute-start.42 = (bf16[4,32,5120]{2,1,0:T(8,128)(2,1)S(1)}, bf16[4,32,5120]{2,1,0:T(8,128)(2,1)S(1)}, u32[]{:S(2)}, u32[]{:S(2)}) collective-permute-start(bf16[4,32,5120]{2,1,0:T(8,128)(2,1)S(1)} %pad_maximum_fusion.4), channel_id=1, source_target_pairs={{0,24},{4,28},{8,0},{12,4},{16,8},{20,12},{24,16},{28,20},{32,56},... | collective-permute-start | bytes 3932168 | tf_op jit(solution)/shard_map/ppermute | solution.py:171
  321.7 30.6 %collective-permute-start.40 = (bf16[4,32,5120]{2,1,0:T(8,128)(2,1)S(1)}, bf16[4,32,5120]{2,1,0:T(8,128)(2,1)S(1)}, u32[]{:S(2)}, u32[]{:S(2)}) collective-permute-start(bf16[4,32,5120]{2,1,0:T(8,128)(2,1)S(1)} %pad_maximum_fusion.3), channel_id=1, source_target_pairs={{0,8},{4,12},{8,16},{12,20},{16,24},{20,28},{24,0},{28,4},{32,40},... | collective-permute-start | bytes 3932168 | tf_op jit(solution)/shard_map/ppermute | solution.py:171
  321.8 27.9 %collective-permute-start.32 = (bf16[16,2560]{1,0:T(8,128)(2,1)S(1)}, bf16[16,2560]{1,0:T(8,128)(2,1)S(1)}, u32[]{:S(2)}, u32[]{:S(2)}) collective-permute-start(bf16[16,2560]{1,0:T(8,128)(2,1)S(1)} %get-tuple-element.109), channel_id=1, source_target_pairs={{0,8},{4,12},{8,16},{12,20},{16,24},{20,28},{24,0},{28,4},{32,40},... | collective-permute-start | bytes 245768 | tf_op jit(solution)/shard_map/ppermute | solution.py:171
  321.9 27.8 %collective-permute-start.34 = (bf16[16,2560]{1,0:T(8,128)(2,1)S(1)}, bf16[16,2560]{1,0:T(8,128)(2,1)S(1)}, u32[]{:S(2)}, u32[]{:S(2)}) collective-permute-start(bf16[16,2560]{1,0:T(8,128)(2,1)S(1)} %get-tuple-element.110), channel_id=1, source_target_pairs={{0,24},{4,28},{8,0},{12,4},{16,8},{20,12},{24,16},{28,20},{32,56},... | collective-permute-start | bytes 245768 | tf_op jit(solution)/shard_map/ppermute | solution.py:171
  325.2 31.1 %collective-permute-start.58 = (bf16[80,960]{1,0:T(8,128)(2,1)S(1)}, bf16[80,960]{1,0:T(8,128)(2,1)S(1)}, u32[]{:S(2)}, u32[]{:S(2)}) collective-permute-start(bf16[80,960]{1,0:T(8,128)(2,1)S(1)} %fusion.37), channel_id=1, source_target_pairs={{0,1},{1,0},{2,3},{3,2},{4,5},{5,4},{6,7},{7,6},{8,9},{9,8},{10,11... | collective-permute-start | bytes 460808 | tf_op jit(solution)/shard_map/ppermute | solution.py:214
  349.7 13.8 %collective-permute-start.35 = (bf16[32,2560]{1,0:T(8,128)(2,1)S(1)}, bf16[32,2560]{1,0:T(8,128)(2,1)S(1)}, u32[]{:S(2)}, u32[]{:S(2)}) collective-permute-start(bf16[32,2560]{1,0:T(8,128)(2,1)S(1)} %pad_maximum_fusion.17), channel_id=1, source_target_pairs={{0,24},{4,28},{8,0},{12,4},{16,8},{20,12},{24,16},{28,20},{32,56},... | collective-permute-start | bytes 491528 | tf_op jit(solution)/shard_map/ppermute | solution.py:171
  361.3 12.4 %collective-permute-start.46 = (bf16[32,5120]{1,0:T(8,128)(2,1)S(1)}, bf16[32,5120]{1,0:T(8,128)(2,1)S(1)}, u32[]{:S(2)}, u32[]{:S(2)}) collective-permute-start(bf16[32,5120]{1,0:T(8,128)(2,1)S(1)} %pad_maximum_fusion.14), channel_id=1, source_target_pairs={{0,96},{4,100},{8,104},{12,108},{16,112},{20,116},{24,120},{28,124... | collective-permute-start | bytes 983048 | tf_op jit(solution)/shard_map/ppermute | solution.py:171
  363.0 10.7 %collective-permute-start.44 = (bf16[32,5120]{1,0:T(8,128)(2,1)S(1)}, bf16[32,5120]{1,0:T(8,128)(2,1)S(1)}, u32[]{:S(2)}, u32[]{:S(2)}) collective-permute-start(bf16[32,5120]{1,0:T(8,128)(2,1)S(1)} %pad_maximum_fusion.13), channel_id=1, source_target_pairs={{0,32},{4,36},{8,40},{12,44},{16,48},{20,52},{24,56},{28,60},{32,6... | collective-permute-start | bytes 983048 | tf_op jit(solution)/shard_map/ppermute | solution.py:171
  (101 other events, 1706.9 us)
Sparse Core Ops, SparseCore 0:
  10.9 69.7 all-gather.1
